TPU v7x, 32 devices: a whole 2x2x4 slice. The times are simulated.
32 devices in a mesh: clips: 4 (over z), ha: 4 (over y, x), wa: 2 (over core).
Axes of the slice: x: 2, y: 2, z: 4, core: 2. Of those that a mesh axis runs over, the one named last changes fastest.
Arguments:
- slow_input: bfloat16 [12, 8, 8, 8, 1024], P('clips', None, 'ha', 'wa'), may hold values from -6 to 6
- fast_input: bfloat16 [12, 32, 8, 8, 128], P('clips', None, 'ha', 'wa'), may hold values from -6 to 6
- slow_cotangent: bfloat16 [12, 8, 8, 8, 1024], P('clips', None, 'ha', 'wa'), may hold values from -6 to 6
- fast_cotangent: bfloat16 [12, 32, 8, 8, 128], P('clips', None, 'ha', 'wa'), may hold values from -6 to 6
- clip_counts: int32 [4], P('clips'), may hold values from 1 to 3, as said below
- lateral_weight: bfloat16 [5, 128, 256], P(None, ('ha', 'wa')), may hold values from -0.25 to 0.25
- slow_reduce_one: bfloat16 [3, 1280, 256], P(None, ('ha', 'wa')), may hold values from -0.09375 to 0.09375
- slow_spatial_one: bfloat16 [3, 3, 256, 256], P(None, None, ('ha', 'wa')), may hold values from -0.125 to 0.125
- slow_expand_one: bfloat16 [256, 1024], P(('ha', 'wa')), may hold values from -0.375 to 0.375
- slow_shortcut_one: bfloat16 [1280, 1024], P(('ha', 'wa')), may hold values from -0.15625 to 0.15625
- fast_reduce_one: bfloat16 [3, 128, 32], P(None, ('ha', 'wa')), may hold values from -0.3125 to 0.3125
- fast_spatial_one: bfloat16 [3, 3, 32, 32], P(None, None, ('ha', 'wa')), may hold values from -0.375 to 0.375
- fast_expand_one: bfloat16 [32, 128], P(('ha', 'wa')), may hold values from -1 to 1
- slow_reduce_two: bfloat16 [3, 1024, 256], P(None, ('ha', 'wa')), may hold values from -0.109375 to 0.109375
- slow_spatial_two: bfloat16 [3, 3, 256, 256], P(None, None, ('ha', 'wa')), may hold values from -0.125 to 0.125
- slow_expand_two: bfloat16 [256, 1024], P(('ha', 'wa')), may hold values from -0.375 to 0.375
- fast_reduce_two: bfloat16 [3, 128, 32], P(None, ('ha', 'wa')), may hold values from -0.3125 to 0.3125
- fast_spatial_two: bfloat16 [3, 3, 32, 32], P(None, None, ('ha', 'wa')), may hold values from -0.375 to 0.375
- fast_expand_two: bfloat16 [32, 128], P(('ha', 'wa')), may hold values from -1 to 1
- slow_norms_one: float32 [2, 2560], replicated, may hold values from -0.75 to 0.75
- fast_norms_one: float32 [2, 192], replicated, may hold values from -0.75 to 0.75
- slow_norms_two: float32 [2, 1536], replicated, may hold values from -0.75 to 0.75
- fast_norms_two: float32 [2, 192], replicated, may hold values from -0.75 to 0.75
Outputs:
- slow_output: bfloat16 [12, 8, 8, 8, 1024], P('clips', None, 'ha', 'wa')
- fast_output: bfloat16 [12, 32, 8, 8, 128], P('clips', None, 'ha', 'wa')
- grad_slow_input: float32 [12, 8, 8, 8, 1024], P('clips', None, 'ha', 'wa')
- grad_fast_input: float32 [12, 32, 8, 8, 128], P('clips', None, 'ha', 'wa')
- grad_lateral_weight: float32 [5, 128, 256], P(None, ('ha', 'wa'))
- grad_slow_reduce_one: float32 [3, 1280, 256], P(None, ('ha', 'wa'))
- grad_slow_spatial_one: float32 [3, 3, 256, 256], P(None, None, ('ha', 'wa'))
- grad_slow_expand_one: float32 [256, 1024], P(('ha', 'wa'))
- grad_slow_shortcut_one: float32 [1280, 1024], P(('ha', 'wa'))
- grad_fast_reduce_one: float32 [3, 128, 32], P(None, ('ha', 'wa'))
- grad_fast_spatial_one: float32 [3, 3, 32, 32], P(None, None, ('ha', 'wa'))
- grad_fast_expand_one: float32 [32, 128], P(('ha', 'wa'))
- grad_slow_reduce_two: float32 [3, 1024, 256], P(None, ('ha', 'wa'))
- grad_slow_spatial_two: float32 [3, 3, 256, 256], P(None, None, ('ha', 'wa'))
- grad_slow_expand_two: float32 [256, 1024], P(('ha', 'wa'))
- grad_fast_reduce_two: float32 [3, 128, 32], P(None, ('ha', 'wa'))
- grad_fast_spatial_two: float32 [3, 3, 32, 32], P(None, None, ('ha', 'wa'))
- grad_fast_expand_two: float32 [32, 128], P(('ha', 'wa'))
- grad_slow_norms_one: float32 [2, 2560], replicated
- grad_fast_norms_one: float32 [2, 192], replicated
- grad_slow_norms_two: float32 [2, 1536], replicated
- grad_fast_norms_two: float32 [2, 192], replicated
Inputs may be any that keep to these rules, and one draw needn't show every extreme that they name: Each group has 3 clip slots, and clip_counts[g] of them, from slot 0, hold clips; some group is full.
All inputs are finite; a program needn't handle non-finite values.
Results may differ from a plain program's by a relative error of at most 0.023.
Values may be sent and summed in bfloat16 or wider, within the bound.
No kernel may reach another device: no remote copies, remote signals or barrier semaphores. Data moves between devices by JAX's collectives and lax.ppermute only.
A program may use at most 128 MiB of HBM per device.

v0:
```python
import jax
import jax.numpy as jnp
from jax import lax
from jax.experimental import pallas as pl
from jax.experimental.pallas import tpu as pltpu
from jax.sharding import PartitionSpec as P

epsilon = 1e-05
F32 = jnp.float32
BF16 = jnp.bfloat16
TILE = ("ha", "wa")
PHASES = 4
SUB = 8


def dot(left, right):
    return lax.dot_general(left, right, (((1,), (0,)), ((), ())), preferred_element_type=F32)


def dot_tn(left, right):
    return lax.dot_general(left, right, (((0,), (0,)), ((), ())), preferred_element_type=F32)


def dot_nt(left, right):
    return lax.dot_general(left, right, (((1,), (1,)), ((), ())), preferred_element_type=F32)


class Keep:
    def __init__(self, ref):
        self.scratch, self.shape = ref, ref.shape

    def send(self):
        pass

    def __setitem__(self, index, value):
        self.scratch[index] = value

    def __getitem__(self, index):
        return self.scratch[index]


class Loads:
    def __init__(self, source, offset, target, sems, first):
        self.copies = []
        depth = target.shape[2]
        for step in range(target.shape[0]):
            copy = pltpu.make_async_copy(
                source.at[:, pl.ds(offset + step * depth, depth), :],
                target.at[step],
                sems.at[first + step],
            )
            copy.start()
            self.copies.append(copy)
        self.target = target

    def get(self, step):
        self.copies[step].wait()
        block = self.target[step]
        return block.reshape(-1, block.shape[-1])


class Saved:
    def __init__(self, source, scratch, sem):
        self.scratch, self.shape = scratch, scratch.shape
        self.copy = pltpu.make_async_copy(source, scratch, sem)
        self.copy.start()
        self.ready = False

    def wait(self):
        if not self.ready:
            self.copy.wait()
            self.ready = True

    def __getitem__(self, index):
        self.wait()
        return self.scratch[index]


SEGMENTS = 8


class Store:
    def __init__(self, scratch, target, sems):
        self.scratch, self.target, self.shape = scratch, target, scratch.shape
        self.sems, self.copies = sems, []

    def send(self):
        self.copies.append(pltpu.make_async_copy(self.scratch, self.target, self.sems[0]))
        self.copies[-1].start()

    def send_rows(self, low, high):
        rows = pl.ds(low, high - low)
        source, target = self.scratch.at[:, rows, :], self.target.at[:, rows, :]
        self.copies.append(pltpu.make_async_copy(source, target, self.sems[len(self.copies)]))
        self.copies[-1].start()

    def __setitem__(self, index, value):
        self.scratch[index] = value

    def __getitem__(self, index):
        return self.scratch[index]


CLOSE = 320 * 1024


def run(body, outs, smem=(), parts=(), vmem=(), saved=(), weights=(), scratch=(), limit=53):
    near = pl.BlockSpec(memory_space=pltpu.VMEM)
    far = pl.BlockSpec(memory_space=pltpu.HBM)
    sources = []
    for array, *_ in weights:
        if not any(array is other for other in sources):
            sources.append(array)
    outs = list(outs) + [(part.shape[1:], part.dtype, "hbm") for part in parts]
    flat = []
    twice = []
    for at, (shape, dtype, kind) in enumerate(outs):
        size = jnp.dtype(dtype).itemsize
        for length in shape:
            size *= length
        twice.append(kind == "both" and size <= CLOSE)
        if kind in ("hbm", "both") and size <= CLOSE:
            outs[at] = (shape, dtype, "vmem")
    for shape, dtype, kind in outs:
        flat += [(shape, dtype, "raw"), (shape, dtype, "vmem")] if kind == "both" else [(shape, dtype, kind)]
    close = [array.size * array.dtype.itemsize <= CLOSE for array in saved]
    held = [pltpu.VMEM(array.shape, array.dtype) for array, here in zip(saved, close) if not here]
    for array, _, steps, depth in weights:
        held.append(pltpu.VMEM((steps, array.shape[0], depth, array.shape[2]), array.dtype))
    for shape, dtype, kind in outs:
        if kind in ("hbm", "rows"):
            held.append(pltpu.VMEM(shape, dtype))
        elif kind == "spread":
            held.append(pltpu.VMEM(shape[1:], dtype))
    sems = len(saved) + sum(steps for _, _, steps, _ in weights) + len(outs)
    sems += SEGMENTS * sum(kind == "rows" for _, _, kind in outs)
    held.append(pltpu.SemaphoreType.DMA((sems,)))

    def kernel(*refs):
        refs = list(refs)

        def take(number):
            taken = refs[:number]
            del refs[:number]
            return taken

        smem_refs, part_refs, vmem_refs = take(len(smem)), take(len(parts)), take(len(vmem))
        saved_refs, source_refs, out_refs = take(len(saved)), take(len(sources)), take(len(flat))
        saved_scratch, weight_scratch = take(len(saved) - sum(close)), take(len(weights))
        out_scratch = take(sum(kind in ("hbm", "rows", "spread") for _, _, kind in outs))
        sem, more = refs[0], refs[1:]
        arrays, copies = [], []
        for source, here in zip(saved_refs, close):
            if not here:
                copies.append(Saved(source, saved_scratch[len(copies)], sem.at[len(copies)]))
            arrays.append(source if here else copies[-1])
        at = len(saved)
        loads = []
        for (array, offset, steps, _), target in zip(weights, weight_scratch):
            place = [array is other for other in sources].index(True)
            loads.append(Loads(source_refs[place], offset, target, sem, at))
            at += steps
        results, stores, spreads = [], [], []
        for _, _, kind in outs:
            ref = out_refs.pop(0)
            if kind == "both":
                stores.append(Store(out_refs.pop(0), ref, [sem.at[at]]))
                at += 1
                results.append(stores[-1])
            elif kind in ("hbm", "rows"):
                number = SEGMENTS if kind == "rows" else 1
                stores.append(
                    Store(out_scratch.pop(0), ref, [sem.at[at + part] for part in range(number)])
                )
                at += number
                results.append(stores[-1])
            elif kind == "spread":
                spreads.append((out_scratch.pop(0), ref))
                results.append(spreads[-1][0])
            elif kind == "vmem":
                results.append(Keep(ref))
            else:
                results.append(ref)
        sums = results[len(results) - len(parts) :]
        results = results[: len(results) - len(parts)]
        for part, total in zip(part_refs, sums):
            total[...] = jnp.sum(part[...], axis=0)
            total.send()
        totals = [total.scratch for total in sums]
        body(*smem_refs, *totals, *vmem_refs, *arrays, *loads, *results, *more)
        for copy in copies:
            copy.wait()
        for store in stores:
            if not store.copies:
                store.send()
        for value, ref in spreads:
            ref[...] = jnp.broadcast_to(value[...][None], ref.shape)
        for store in stores:
            for copy in store.copies:
                copy.wait()

    results = pl.pallas_call(
        kernel,
        out_shape=[jax.ShapeDtypeStruct(shape, dtype) for shape, dtype, _ in flat],
        in_specs=[pl.BlockSpec(memory_space=pltpu.SMEM)] * len(smem)
        + [near] * (len(parts) + len(vmem))
        + [near if here else far for here in close]
        + [far] * len(sources),
        out_specs=[far if kind in ("hbm", "rows", "raw") else near for _, _, kind in flat],
        scratch_shapes=held + list(scratch),
        compiler_params=pltpu.CompilerParams(vmem_limit_bytes=limit * 1024 * 1024),
        cost_estimate=pl.CostEstimate(
            flops=2_000_000_000, bytes_accessed=16_000_000, transcendentals=0
        ),
    )(*smem, *parts, *vmem, *saved, *sources)
    returned = []
    for (_, _, kind), double in zip(outs, twice):
        taken, results = results[: 2 if kind == "both" else 1], results[2 if kind == "both" else 1 :]
        returned += list(taken) * (2 if double else 1)
    return returned


class Geometry:
    def __init__(self, slow_shape, fast_shape):
        self.cap, self.frames, self.height, self.width = slow_shape[:4]
        self.groups = self.cap * self.frames
        self.rows = self.groups * SUB

    def three(self, value):
        return value.reshape(-1, SUB, value.shape[-1])

    def flat(self, value):
        return value.reshape(-1, value.shape[-1])

    def shift(self, value, step):
        lanes = value.shape[-1]
        whole = value.reshape(self.cap, self.frames, SUB, lanes)
        zero = jnp.zeros((self.cap, 1, SUB, lanes), value.dtype)
        if step > 0:
            whole = jnp.concatenate([zero, whole[:, :-1]], axis=1)
        else:
            whole = jnp.concatenate([whole[:, 1:], zero], axis=1)
        return whole.reshape(-1, lanes)


def mask_groups(shape, limit, scale=1):
    return lax.broadcasted_iota(jnp.int32, shape, 0) * scale < limit


def rep(ref, row, low, high):
    return jnp.broadcast_to(ref[row : row + 1, low:high], (SUB, high - low))


def fold(value, slow):
    fast = value[:, slow:]
    lanes = fast.shape[-1]
    part = lanes // PHASES
    if part % 128 == 0:
        total = fast[:, :part]
        for phase in range(1, PHASES):
            total = total + fast[:, phase * part : (phase + 1) * part]
        return jnp.concatenate([value[:, :slow]] + [total] * PHASES, axis=1)
    total = fast
    for phase in range(1, PHASES):
        total = total + pltpu.roll(fast, phase * part, 1)
    return jnp.concatenate([value[:, :slow], total], axis=1)


def lane_counts(inv_ref, lanes, slow):
    lane = lax.broadcasted_iota(jnp.int32, (SUB, lanes), 1)
    return jnp.where(lane < slow, inv_ref[0], inv_ref[1])


def moments(stats, inv_ref, slow, low=0, high=None):
    high = stats.shape[1] if high is None else high
    total, square = rep(stats, 0, low, high), rep(stats, 1, low, high)
    if slow < high - low:
        total, square = fold(total, slow), fold(square, slow)
    inv_n = lane_counts(inv_ref, high - low, slow)
    mean = total * inv_n
    return mean, lax.rsqrt(square * inv_n - mean * mean + epsilon)


def affine(stats, params, inv_ref, slow, low=0, high=None):
    mean, inv = moments(stats, inv_ref, slow, low, high)
    lanes = mean.shape[1]
    scale = (1.0 + rep(params, 0, 0, lanes)) * inv
    return scale, rep(params, 1, 0, lanes) - mean * scale, mean, inv


def back_rows(sums, inv_ref, slow, row, low=0, high=None):
    high = sums.shape[1] if high is None else high
    total = rep(sums, row, low, high)
    if slow < high - low:
        total = fold(total, slow)
    return total * lane_counts(inv_ref, high - low, slow)


def silu(value):
    return value * jax.nn.sigmoid(value)


def slope(value):
    sigma = jax.nn.sigmoid(value)
    return sigma * (1.0 + value * (1.0 - sigma))


def put_stats(ref, first, second, low=0):
    lanes = first.shape[-1]
    ref[0:1, low : low + lanes] = jnp.sum(jnp.sum(first, axis=0), axis=0, keepdims=True)
    ref[1:2, low : low + lanes] = jnp.sum(jnp.sum(second, axis=0), axis=0, keepdims=True)


def put_back(ref, gradient, normal, low=0):
    put_stats(ref, gradient * normal, gradient, low)


def put_forward(ref, value, limit, low=0):
    masked = jnp.where(mask_groups(value.shape, limit), value, 0.0)
    put_stats(ref, masked, masked * value, low)


EDGE = 32


def edge_place(wa, width):
    return jnp.where(wa > 0, 0, width - 1)


def put_message(value, ref, edge_ref, meta_ref, width):
    lanes = value.shape[-1]
    pairs = value.reshape(-1, 2, SUB, lanes)
    first, second = pairs[:, 0], pairs[:, 1]
    near = lax.broadcasted_iota(jnp.int32, first.shape, 1) < SUB // 2
    top = jnp.where(near, first, pltpu.roll(second, SUB // 2, 1))
    bottom = jnp.where(near, pltpu.roll(first, SUB // 2, 1), second)
    flat = value.reshape(-1, lanes).astype(BF16)
    shape = (2 * EDGE, flat.shape[0])
    row, col = [lax.broadcasted_iota(jnp.int32, shape, dim) for dim in range(2)]
    low = row >= EDGE
    source = (row - jnp.where(low, EDGE, 0)) * SUB + jnp.where(low, SUB // 2, 0)
    chosen = (col == source + edge_place(meta_ref[2], width)).astype(F32).astype(BF16)
    edges = dot(chosen, flat)
    edge_ref[...] = edges.astype(BF16)
    edge_ref.send()
    top, bottom = [part.reshape(-1, lanes).astype(BF16) for part in (top, bottom)]
    ref[: top.shape[0]] = top
    ref[top.shape[0] :] = bottom
    ref.send()


def unpack_bottom(value):
    both = jnp.stack([pltpu.roll(value, SUB // 2, 1), value], axis=1)
    return both.reshape(-1, SUB, value.shape[-1])


def unpack_top(value):
    both = jnp.stack([value, pltpu.roll(value, SUB // 2, 1)], axis=1)
    return both.reshape(-1, SUB, value.shape[-1])


class Neighbours:
    def __init__(self, own, up, down, edges, meta, width):
        half = SUB // 2
        near = lax.broadcasted_iota(jnp.int32, own.shape, 1) < half
        self.col = lax.broadcasted_iota(jnp.int32, own.shape, 1) % width
        self.width, self.shape = width, own.shape
        ha, wa, last = meta[1], meta[2], meta[3]
        up = unpack_bottom(jnp.where(ha > 0, up, 0.0))
        down = unpack_top(jnp.where(ha < last, down, 0.0))
        self.rows = {
            0: own,
            -1: pltpu.roll(jnp.where(near, own, up), half, 1),
            1: pltpu.roll(jnp.where(near, down, own), half, 1),
        }
        beyond = lax.broadcasted_iota(jnp.int32, edges.shape, 0)
        inside = ((ha > 0) | (beyond >= EDGE)) & ((ha < last) | (beyond < 3 * EDGE))
        self.edges = jnp.where(inside, edges, 0.0).astype(BF16)
        shape = (own.shape[0] * SUB, edges.shape[0])
        place, self.source = [lax.broadcasted_iota(jnp.int32, shape, dim) for dim in range(2)]
        self.group = place // SUB
        self.row = place // half % 2
        self.touches = place % width == edge_place(wa, width)
        self.sides = {}

    def side(self, row_step):
        if row_step not in self.sides:
            wanted = (self.row + row_step + 1) * EDGE + self.group
            chosen = ((self.source == wanted) & self.touches).astype(F32).astype(BF16)
            self.sides[row_step] = dot(chosen, self.edges).reshape(self.shape)
        return self.sides[row_step]

    def at(self, row_step, col_step):
        base = self.rows[row_step]
        if col_step < 0:
            return jnp.where(self.col == 0, self.side(row_step), pltpu.roll(base, 1, 1))
        if col_step > 0:
            away = self.col == self.width - 1
            return jnp.where(away, self.side(row_step), pltpu.roll(base, SUB - 1, 1))
        return base


def xor_pairs(size, step):
    return [(index, index ^ step) for index in range(size)]


def direct_sum(value, axis):
    size = lax.axis_size(axis)
    step = 1
    while step < size:
        if size // step >= 4:
            one, two, three = [
                lax.ppermute(value, axis, xor_pairs(size, step * times)) for times in (1, 2, 3)
            ]
            value = (value + two) + (one + three)
            step *= 4
        else:
            value = value + lax.ppermute(value, axis, xor_pairs(size, step))
            step *= 2
    return value


AXES = ("clips", "ha", "wa")
MOST = 32


def spread_count():
    count = lax.axis_size("ha") * lax.axis_size("wa")
    whole = count * lax.axis_size("clips")
    return whole if whole <= MOST else count


def exchange(copies):
    if copies.shape[0] == lax.axis_size("clips") * lax.axis_size("ha") * lax.axis_size("wa"):
        return lax.all_to_all(copies, AXES, 0, 0)
    return lax.all_to_all(direct_sum(copies, "clips"), TILE, 0, 0)


def exchange_widest(sums):
    count = lax.axis_size("ha") * lax.axis_size("wa")
    sums = direct_sum(sums, "clips")
    return lax.all_to_all(jnp.broadcast_to(sums[None], (count,) + sums.shape), TILE, 0, 0)


def exchange_halo(message, edges):
    wide, high = lax.axis_size("wa"), lax.axis_size("ha")
    half = message.shape[0] // 2
    side = lax.ppermute(edges, "wa", xor_pairs(wide, 1))
    odd = lax.axis_index("ha") % 2 == 1
    tops = jnp.concatenate([message[:half], side[:EDGE]], axis=0)
    bottoms = jnp.concatenate([message[half:], side[EDGE:]], axis=0)
    first = lax.ppermute(jnp.where(odd, tops, bottoms), "ha", xor_pairs(high, 1))
    pairs = [(row, row + 1) for row in range(1, high - 1, 2)]
    pairs = pairs + [(low, row) for row, low in pairs]
    second = lax.ppermute(jnp.where(odd, bottoms, tops), "ha", pairs)
    return side, first, second


def from_above_and_below(first_ref, second_ref, meta_ref):
    first, second = first_ref[...].astype(F32), second_ref[...].astype(F32)
    odd = meta_ref[1] % 2 == 1
    return jnp.where(odd, first, second), jnp.where(odd, second, first)


def time_conv(geo, parts, blocks):
    result = None
    for tap in range(3):
        at = 0
        total = None
        for part in parts:
            lanes = part.shape[-1]
            term = dot(part, blocks[tap][at : at + lanes])
            at += lanes
            total = term if total is None else total + term
        if tap != 1:
            total = geo.shift(total, 1 - tap)
        result = total if result is None else result + total
    return result


def fast_conv(geo, value, main, before, after):
    lanes = value.shape[-1] // PHASES
    result = dot(value, main)
    result = result + geo.shift(dot(value[:, -lanes:], before), 1)
    return result + geo.shift(dot(value[:, :lanes], after), -1)


def fast_conv_back(steps, main, before, after):
    lanes = before.shape[0]
    middle = dot_nt(steps[1], main)
    first = middle[:, :lanes] + dot_nt(steps[2], after)
    last = middle[:, -lanes:] + dot_nt(steps[0], before)
    return jnp.concatenate([first, middle[:, lanes:-lanes], last], axis=1)


def lane_block(value, phase, part):
    return pltpu.roll(value, value.shape[-1] - phase * part, 1) if phase else value


def fast_reduce_grad(value, steps):
    lanes = value.shape[-1] // PHASES
    part = steps[1].shape[-1] // PHASES
    main = dot_tn(value, steps[1])
    before = dot_tn(value[:, -lanes:], steps[0])
    after = dot_tn(value[:, :lanes], steps[2])

    def block(row, col):
        return lane_block(main[row * lanes : (row + 1) * lanes], col, part)

    result = []
    for tap in range(3):
        total = before if tap == 0 else None
        if tap == 2:
            total = lane_block(after, PHASES - 1, part)
        for col in range(PHASES):
            row = col + tap - 1
            if 0 <= row < PHASES:
                total = block(row, col) if total is None else total + block(row, col)
        result.append(total)
    return result


def gather_pack(parts):
    return lax.all_gather(jnp.concatenate(parts, axis=0), TILE, axis=0)


def columns(shard, lanes):
    depth, total = shard.shape
    return jnp.moveaxis(shard.reshape(depth, total // lanes, lanes), 1, 0).reshape(-1, lanes)


def split_phases(value):
    cap, frames, height, width, lanes = value.shape
    value = value.reshape(cap, frames // PHASES, PHASES, height, width, lanes)
    return jnp.moveaxis(value, 2, 4).reshape(-1, PHASES * lanes)


def join_phases(value, shape):
    cap, frames, height, width, lanes = shape
    value = value.reshape(cap, frames // PHASES, height, width, PHASES, lanes)
    return jnp.moveaxis(value, 4, 2).reshape(shape)


def early_gather(shards_one, shards_two, lateral):
    rows = []
    lanes = shards_one[2].shape[-1]
    kinds = [jnp.stack(pair) for pair in zip(shards_one, shards_two)]
    kinds.append(jnp.stack([lateral[..., :lanes], lateral[..., lanes:]]))
    for kind in kinds:
        flat = kind.reshape(-1, kind.shape[-1])
        rows.append(jnp.pad(flat, ((0, 0), (0, lanes - flat.shape[-1]))))
    packed = gather_pack(rows)
    result = []
    at = 0
    for kind in kinds:
        depth, width = kind.shape[-2:]
        number = kind.size // width
        part = packed[:, at : at + number, :width].reshape(packed.shape[0], -1, depth, width)
        at += number
        result.append(jnp.moveaxis(part, 0, 1).reshape(part.shape[1], -1, width))
    return result


def prepare_kernel(taps_ref, space_ref, wide_ref, lateral_ref, *refs):
    slow_one, fast_one, slow_two, fast_two, *outs = refs
    part = taps_ref.shape[-1]
    lateral, *joint = outs[10:]
    number = lateral.shape[0]
    for tap in range(number):
        lateral[tap] = jnp.concatenate([lateral_ref[tap], lateral_ref[number + tap]], axis=1)
    for layer, (slow, fast) in enumerate(((slow_one, fast_one), (slow_two, fast_two))):
        at = fast_at = 0
        for ref in joint[3 * layer : 3 * layer + 3]:
            fast_lanes = part if ref.shape[1] < slow.shape[1] // 2 else wide_ref.shape[-1]
            lanes = ref.shape[1] - PHASES * fast_lanes
            values = [slow[:, at : at + lanes]]
            values += [fast[:, fast_at : fast_at + fast_lanes]] * PHASES
            ref[...] = jnp.concatenate(values, axis=1)
            at, fast_at = at + lanes, fast_at + fast_lanes
    joint[6][...] = slow_one[:, slow_one.shape[1] - joint[6].shape[1] :]
    for layer in range(2):
        main, before, after, space, wide = outs[5 * layer : 5 * layer + 5]
        taps = [taps_ref[3 * layer + tap] for tap in range(3)]
        zero = jnp.zeros_like(taps[0])
        lanes = taps[0].shape[0]
        for row in range(PHASES):
            blocks = [
                taps[row - col + 1] if abs(row - col) <= 1 else zero for col in range(PHASES)
            ]
            main[row * lanes : (row + 1) * lanes, :] = jnp.concatenate(blocks, axis=1)
        before[...] = jnp.concatenate([taps[0]] + [zero] * (PHASES - 1), axis=1)
        after[...] = jnp.concatenate([zero] * (PHASES - 1) + [taps[2]], axis=1)
        for tap in range(9):
            block = space_ref[9 * layer + tap]
            none = jnp.zeros_like(block)
            for row in range(PHASES):
                blocks = [block if row == col else none for col in range(PHASES)]
                space[tap, row * part : (row + 1) * part, :] = jnp.concatenate(blocks, axis=1)
        block = wide_ref[layer]
        none = jnp.zeros_like(block)
        for row in range(PHASES):
            blocks = [block if row == col else none for col in range(PHASES)]
            wide[row * part : (row + 1) * part, :] = jnp.concatenate(blocks, axis=1)


def to_partners(pieces, axis):
    size = lax.axis_size(axis)
    return [
        lax.ppermute(piece, axis, xor_pairs(size, step + 1)) for step, piece in enumerate(pieces)
    ]


def clip_parts(meta, groups, number):
    lanes = groups[0][0].shape[1]
    lengths = [group[0].shape[0] for group in groups]
    depth = sum(lengths) // number
    total_ins = sum(len(group) for group in groups)

    def kernel(meta_ref, *refs):
        ins, outs, total_ref = list(refs[:total_ins]), refs[total_ins:-1], refs[-1]
        at = 0
        for group, length in zip(groups, lengths):
            mine, ins = ins[: len(group)], ins[len(group) :]
            total = mine[0][...]
            if len(mine) > 1:
                total = total.astype(F32)
                for ref in mine[1:]:
                    total = total + ref[...].astype(F32)
                total = total.astype(BF16)
            total_ref[at : at + length, :] = total
            at += length
        for step, out in enumerate(outs):
            start = pl.multiple_of((meta_ref[4] ^ step) * depth, 16) if number > 1 else 0
            out[...] = total_ref[pl.ds(start, depth), :]
            out.send()

    return run(
        kernel,
        [((depth, lanes), BF16, "hbm")] * number,
        smem=(meta,),
        saved=[part for group in groups for part in group],
        scratch=(pltpu.VMEM((sum(lengths), lanes), BF16),),
    )


def add_low(first, *others):
    total = first.astype(F32)
    for other in others:
        total = total + other.astype(F32)
    return total.astype(BF16)


def on_device(
    slow_input,
    fast_input,
    slow_cotangent,
    fast_cotangent,
    clip_counts,
    lateral_weight,
    slow_reduce_one,
    slow_spatial_one,
    slow_expand_one,
    slow_shortcut_one,
    fast_reduce_one,
    fast_spatial_one,
    fast_expand_one,
    slow_reduce_two,
    slow_spatial_two,
    slow_expand_two,
    fast_reduce_two,
    fast_spatial_two,
    fast_expand_two,
    slow_norms_one,
    fast_norms_one,
    slow_norms_two,
    fast_norms_two,
):
    geo = Geometry(slow_input.shape, fast_input.shape)
    rows, groups = geo.rows, geo.groups
    half_rows = rows // 2
    count = lax.axis_size("ha") * lax.axis_size("wa")
    spread = spread_count()
    slow_wide = slow_input.shape[-1]
    fast_wide = PHASES * fast_input.shape[-1]
    wide = slow_wide + fast_wide
    mid = slow_reduce_one.shape[-1]
    fast_part = fast_reduce_one.shape[-1]
    fast_mid = PHASES * fast_part
    small = mid + fast_mid
    lat = lateral_weight.shape[-1]
    blocks = slow_wide // mid

    depth_one = slow_reduce_one.shape[1]
    depth_two = slow_reduce_two.shape[1]
    depth_mid = slow_spatial_one.shape[2]
    depth_lat = lateral_weight.shape[1]
    near = gather_pack([slow_reduce_one.reshape(-1, mid), slow_spatial_one.reshape(-1, mid)])
    far = gather_pack(
        [
            columns(slow_expand_one, mid),
            columns(slow_shortcut_one, mid),
            slow_reduce_two.reshape(-1, mid),
        ]
    )
    last = gather_pack([slow_spatial_two.reshape(-1, mid), columns(slow_expand_two, mid)])
    at_space_one = 3 * depth_one
    at_short = blocks * depth_mid
    at_reduce_two = at_short + blocks * depth_one
    at_space_two = 0
    at_expand_two = 9 * depth_mid
    fast_shards_one = (fast_reduce_one, fast_spatial_one, fast_expand_one)
    fast_shards_two = (fast_reduce_two, fast_spatial_two, fast_expand_two)
    compact = early_gather(fast_shards_one, fast_shards_two, lateral_weight)
    structured = [
        ((fast_wide, fast_mid), BF16, "hbm"),
        ((fast_wide // PHASES, fast_mid), BF16, "hbm"),
        ((fast_wide // PHASES, fast_mid), BF16, "hbm"),
        ((9, fast_mid, fast_mid), BF16, "hbm"),
        ((fast_mid, fast_wide), BF16, "hbm"),
    ]
    joint_outs = [((2, lanes), F32, "hbm") for lanes in (small, small, wide)]
    prepared = run(
        prepare_kernel,
        structured * 2
        + [((lateral_weight.shape[0], fast_wide // PHASES, lat), BF16, "hbm")]
        + joint_outs * 2
        + [((2, slow_wide), F32, "hbm")],
        vmem=(*compact, slow_norms_one, fast_norms_one, slow_norms_two, fast_norms_two),
    )
    fast_one, fast_two, lateral = prepared[:5], prepared[5:10], prepared[10]
    params_one, params_two, params_short = prepared[11:14], prepared[14:17], prepared[17]

    held = clip_counts[0]
    clips = direct_sum(jnp.full((1, 128), held, F32), "clips")[0, 0]
    positions = clips * (SUB * geo.frames * count)
    inv_n = jnp.stack([1.0 / positions, 1.0 / (positions * PHASES)])
    ha, wa = lax.axis_index("ha"), lax.axis_index("wa")
    last_ha = jnp.full_like(ha, lax.axis_size("ha") - 1)
    meta = jnp.stack([held * geo.frames, ha, wa, last_ha, lax.axis_index("clips")])
    scalars = (meta, inv_n)

    slow_x = slow_input.reshape(rows, slow_wide)
    fast_x = split_phases(fast_input)
    cot = jnp.concatenate(
        [slow_cotangent.reshape(rows, slow_wide), split_phases(fast_cotangent)], axis=1
    )
    message_out = [((rows, small), BF16, "hbm"), ((2 * EDGE, small), BF16, "hbm")]
    stats_small = ((spread, 2, small), F32, "spread")
    stats_wide = ((spread, 2, wide), F32, "spread")
    stats_both = ((2, wide + slow_wide), F32, "vmem")
    small_out = ((rows, small), F32, "hbm")
    wide_out = ((rows, wide), F32, "hbm")
    small_both = ((rows, small), F32, "both")
    small_next = ((rows, small), F32, "vmem")
    wide_low = ((rows, wide), BF16, "hbm")

    def lateral_kernel(x_ref, k_ref, main_ref, before_ref, after_ref, united_ref, fast_ref):
        lanes = x_ref.shape[1] // PHASES
        x = x_ref[...]
        main = dot(x[:, : 3 * lanes], k_ref[2:5].reshape(3 * lanes, lat))
        past = dot(x[:, 2 * lanes :], k_ref[0:2].reshape(2 * lanes, lat))
        united_ref[...] = (main + geo.shift(past, 1)).astype(BF16)
        fast_ref[...] = fast_conv(geo, x, main_ref[...], before_ref[...], after_ref[...])

    united, za_fast = run(
        lateral_kernel,
        [((rows, lat), BF16, "hbm"), ((rows, fast_mid), F32, "hbm")],
        saved=(fast_x, lateral, *fast_one[:3]),
    )

    def reduce_one_kernel(
        meta_ref, x_ref, united_ref, fast_ref, loads, za_ref, stats_ref, message_ref, edge_ref
    ):
        weights = [loads.get(tap) for tap in range(3)]
        za = time_conv(geo, (x_ref[...], united_ref[...]), weights)
        za = jnp.concatenate([za, fast_ref[...]], axis=1)
        za_ref[...] = za
        za_ref.send()
        za = geo.three(za)
        put_message(za, message_ref, edge_ref, meta_ref, geo.width)
        put_forward(stats_ref, za, meta_ref[0])

    za_one, za_next, stats, message, edges = run(
        reduce_one_kernel,
        [small_both, stats_small, *message_out],
        smem=(meta,),
        saved=(slow_x, united, za_fast),
        weights=((near, 0, 3, depth_one),),
    )
    parts_a1 = exchange(stats)
    halo_one = exchange_halo(message, edges)

    def space_stage(za, parts_a, halo, params, gathered, offset, fast_w):
        def kernel(
            meta_ref,
            inv_ref,
            stats_ref,
            za_ref,
            side_ref,
            up_ref,
            down_ref,
            params_ref,
            fast_ref,
            loads,
            zb_ref,
            hidden_ref,
            out_stats,
        ):
            scale, shift, _, _ = affine(stats_ref, params_ref, inv_ref, mid)

            def act(value):
                return silu(geo.three(value.astype(F32)) * scale + shift)

            own = act(za_ref[...])
            up, down = from_above_and_below(up_ref, down_ref, meta_ref)
            side = side_ref[...].astype(F32)
            edges = jnp.concatenate([up[half_rows:], side, down[half_rows:]], axis=0)
            hidden_ref[...] = geo.flat(own).astype(BF16)
            hidden_ref.send()
            near_by = Neighbours(
                own,
                act(up[:half_rows]),
                act(down[:half_rows]),
                geo.flat(act(edges)),
                meta_ref,
                geo.width,
            )
            slow = fast = None
            for tap in range(9):
                moved = geo.flat(near_by.at(tap // 3 - 1, tap % 3 - 1)).astype(BF16)
                slow_term = dot(moved[:, :mid], loads.get(tap))
                fast_term = dot(moved[:, mid:], fast_ref[tap])
                slow = slow_term if slow is None else slow + slow_term
                fast = fast_term if fast is None else fast + fast_term
            zb = jnp.concatenate([slow, fast], axis=1)
            zb_ref[...] = zb
            zb_ref.send()
            put_forward(out_stats, geo.three(zb), meta_ref[0])

        zb, zb_next, hidden, stats, stats_a = run(
            kernel,
            [small_both, ((rows, small), BF16, "hbm"), stats_small],
            smem=scalars,
            parts=(parts_a,),
            vmem=(za,),
            saved=(*halo, params, fast_w),
            weights=((gathered, offset, 9, depth_mid),),
        )
        return zb, zb_next, hidden, exchange(stats), stats_a

    zb_one, zb_next, ha_one, parts_b1, stats_a1 = space_stage(
        za_next, parts_a1, halo_one, params_one[0], near, at_space_one, fast_one[3]
    )

    def expand_body(
        inv_ref, stats_ref, zb_ref, params_ref, fast_ref, hidden_ref, low_ref, zc_ref, loads
    ):
        scale, shift, _, _ = affine(stats_ref, params_ref, inv_ref, mid)
        hidden = geo.flat(silu(geo.three(zb_ref[...]) * scale + shift)).astype(BF16)
        hidden_ref[...] = hidden
        hidden_ref.send()
        zc_ref[:, slow_wide:] = dot(hidden[:, mid:], fast_ref[...])
        for block in range(blocks):
            zc_ref[:, block * mid : (block + 1) * mid] = dot(hidden[:, :mid], loads.get(block))
        low_ref[...] = zc_ref[...].astype(BF16)
        low_ref.send()

    def expand_one_kernel(
        meta_ref,
        inv_ref,
        stats_ref,
        zb_ref,
        params_ref,
        fast_ref,
        x_ref,
        united_ref,
        loads,
        shorts,
        hidden_ref,
        low_ref,
        short_low_ref,
        out_stats,
        zc_ref,
        short_ref,
    ):
        expand_body(
            inv_ref, stats_ref, zb_ref, params_ref, fast_ref, hidden_ref, low_ref, zc_ref, loads
        )
        put_forward(out_stats, geo.three(zc_ref[...]), meta_ref[0])
        for block in range(blocks):
            weight = shorts.get(block)
            value = dot(x_ref[...], weight[:slow_wide]) + dot(united_ref[...], weight[slow_wide:])
            short_ref[:, block * mid : (block + 1) * mid] = value
            put_forward(out_stats, geo.three(value), meta_ref[0], wide + block * mid)
        short_low_ref[...] = short_ref[...].astype(BF16)
        short_low_ref.send()

    hb_one, zc_one, short, stats, stats_b1 = run(
        expand_one_kernel,
        [
            ((rows, small), BF16, "hbm"),
            wide_low,
            ((rows, slow_wide), BF16, "hbm"),
            stats_both,
        ],
        scratch=(pltpu.VMEM((rows, wide), F32), pltpu.VMEM((rows, slow_wide), F32)),
        smem=scalars,
        parts=(parts_b1,),
        vmem=(zb_next,),
        saved=(params_one[1], fast_one[4], slow_x, united),
        weights=((far, 0, blocks, depth_mid), (far, at_short, blocks, depth_one)),
    )
    parts_c1 = exchange_widest(stats)

    def reduce_two_kernel(
        meta_ref,
        inv_ref,
        stats_ref,
        zc_ref,
        short_ref,
        params_ref,
        short_params_ref,
        x_ref,
        main_ref,
        before_ref,
        after_ref,
        loads,
        sum_ref,
        low_ref,
        za_ref,
        out_stats,
        message_ref,
        edge_ref,
    ):
        scale, shift, _, _ = affine(stats_ref, params_ref, inv_ref, slow_wide, 0, wide)
        scale_s, shift_s, _, _ = affine(
            stats_ref, short_params_ref, inv_ref, slow_wide, wide, wide + slow_wide
        )
        normed = geo.three(zc_ref[...].astype(F32)) * scale + shift
        slow = normed[..., :slow_wide] + (
            geo.three(short_ref[...].astype(F32)) * scale_s + shift_s
        )
        fast = normed[..., slow_wide:] + geo.three(x_ref[...].astype(F32))
        total = jnp.concatenate([slow, fast], axis=-1)
        sum_ref[...] = geo.flat(total).astype(BF16)
        sum_ref.send()
        low = geo.flat(silu(total)).astype(BF16)
        low_ref[...] = low
        low_ref.send()
        weights = [loads.get(tap) for tap in range(3)]
        za = time_conv(geo, (low[:, :slow_wide],), weights)
        fast_za = fast_conv(
            geo, low[:, slow_wide:], main_ref[...], before_ref[...], after_ref[...]
        )
        za = jnp.concatenate([za, fast_za], axis=1)
        za_ref[...] = za
        za_ref.send()
        za = geo.three(za)
        put_message(za, message_ref, edge_ref, meta_ref, geo.width)
        put_forward(out_stats, za, meta_ref[0])

    sum_one, low_one, za_two, za_next, stats, message, edges, stats_c1 = run(
        reduce_two_kernel,
        [wide_low, wide_low, small_both, stats_small, *message_out],
        smem=scalars,
        parts=(parts_c1,),
        saved=(zc_one, short, params_one[2], params_short, fast_x, *fast_two[:3]),
        weights=((far, at_reduce_two, 3, depth_two),),
    )
    parts_a2 = exchange(stats)
    halo_two = exchange_halo(message, edges)
    zb_two, zb_next, ha_two, parts_b2, stats_a2 = space_stage(
        za_next, parts_a2, halo_two, params_two[0], last, at_space_two, fast_two[3]
    )

    def expand_two_kernel(
        meta_ref,
        inv_ref,
        stats_ref,
        zb_ref,
        params_ref,
        fast_ref,
        loads,
        hidden_ref,
        low_ref,
        out_stats,
        zc_ref,
    ):
        expand_body(
            inv_ref, stats_ref, zb_ref, params_ref, fast_ref, hidden_ref, low_ref, zc_ref, loads
        )
        put_forward(out_stats, geo.three(zc_ref[...]), meta_ref[0])

    hb_two, zc_two, stats, stats_b2 = run(
        expand_two_kernel,
        [((rows, small), BF16, "hbm"), wide_low, stats_wide],
        scratch=(pltpu.VMEM((rows, wide), F32),),
        smem=scalars,
        parts=(parts_b2,),
        vmem=(zb_next,),
        saved=(params_two[1], fast_two[4]),
        weights=((last, at_expand_two, blocks, depth_mid),),
    )
    parts_c2 = exchange(stats)

    def head_kernel(
        meta_ref,
        inv_ref,
        stats_ref,
        zc_ref,
        params_ref,
        sum_ref,
        cot_ref,
        out_ref,
        low_ref,
        sums_ref,
    ):
        scale, shift, mean, inv = affine(stats_ref, params_ref, inv_ref, slow_wide)
        zc = geo.three(zc_ref[...].astype(F32))
        total = zc * scale + shift + silu(geo.three(sum_ref[...].astype(F32)))
        valid = mask_groups(total.shape, meta_ref[0])
        sigma = jax.nn.sigmoid(total)
        out_ref[...] = geo.flat(jnp.where(valid, total * sigma, 0.0)).astype(BF16)
        slopes = sigma * (1.0 + total * (1.0 - sigma))
        gradient = jnp.where(valid, geo.three(cot_ref[...].astype(F32)) * slopes, 0.0)
        out_ref.send()
        low_ref[...] = geo.flat(gradient).astype(BF16)
        low_ref.send()
        put_back(sums_ref, gradient, (zc - mean) * inv)

    outputs, g_two, sums, stats_c2 = run(
        head_kernel,
        [((rows, wide), BF16, "hbm"), wide_low, stats_wide],
        smem=scalars,
        parts=(parts_c2,),
        saved=(zc_two, params_two[2], sum_one, cot),
    )
    parts_c2 = exchange(sums)

    def norm_back(gradient, value, coeffs, sums, valid):
        scale, _, mean, inv = coeffs
        crossed = (value - mean) * inv * sums[0] + sums[1]
        return scale * (gradient - jnp.where(valid, crossed, 0.0))

    def expand_back_body(
        meta_ref,
        inv_ref,
        sums_ref,
        g_ref,
        stats_ref,
        stats_b_ref,
        zc_ref,
        params_ref,
        zb_ref,
        params_b_ref,
        fast_ref,
        loads,
        gz_ref,
        g_out,
        sums_out,
        message_ref,
        edge_ref,
    ):
        limit = meta_ref[0]
        coeffs = affine(stats_ref, params_ref, inv_ref, slow_wide, 0, wide)
        both = [back_rows(sums_ref, inv_ref, slow_wide, row, 0, wide) for row in range(2)]
        gradient = geo.three(g_ref[...].astype(F32))
        gz = norm_back(
            gradient,
            geo.three(zc_ref[...].astype(F32)),
            coeffs,
            both,
            mask_groups(gradient.shape, limit),
        )
        gz = geo.flat(gz).astype(BF16)
        gz_ref[...] = gz
        gz_ref.send()
        fast = dot_nt(gz[:, slow_wide:], fast_ref[...])
        slow = None
        for block in range(blocks):
            term = dot_nt(gz[:, block * mid : (block + 1) * mid], loads.get(block))
            slow = term if slow is None else slow + term
        scale, shift, mean, inv = affine(stats_b_ref, params_b_ref, inv_ref, mid)
        zb = geo.three(zb_ref[...])
        back = geo.three(jnp.concatenate([slow, fast], axis=1)) * slope(zb * scale + shift)
        g_out[...] = geo.flat(back)
        put_message(
            jnp.concatenate([back, zb], axis=-1), message_ref, edge_ref, meta_ref, geo.width
        )
        masked = jnp.where(mask_groups(back.shape, limit), back, 0.0)
        put_back(sums_out, masked, (zb - mean) * inv)
        return gradient

    message_back = [((rows, 2 * small), BF16, "hbm"), ((2 * EDGE, 2 * small), BF16, "hbm")]
    gz_c2, g_b2, sums, message, edges, sums_c2 = run(
        expand_back_body,
        [((rows, wide), BF16, "hbm"), small_next, stats_small, *message_back],
        smem=scalars,
        parts=(parts_c2,),
        saved=(g_two, stats_c2, stats_b2, zc_two, params_two[2], zb_two, params_two[1], fast_two[4]),
        weights=((last, at_expand_two, blocks, depth_mid),),
    )
    parts_b2 = exchange(sums)
    halo_back_two = exchange_halo(message, edges)
    align = 16 * lax.axis_size("clips")

    def aligned(number):
        return number + -number % align


    lanes_fast = fast_wide // PHASES
    fast_rows_count = fast_reduce_one.shape[1] + 2 * SUB

    def expand_grad(hb_ref, gz_ref, out_ref, at):
        for block in range(blocks):
            value = dot_tn(hb_ref[:, :mid], gz_ref[:, block * mid : (block + 1) * mid])
            low = at + block * depth_mid
            out_ref[:, low : low + depth_mid, :] = value.astype(BF16).reshape(
                count, depth_mid, mid
            )
        if isinstance(out_ref, Store):
            out_ref.send_rows(at, at + blocks * depth_mid)

    def fast_expand_grad(hb_ref, gz_ref):
        fast = dot_tn(hb_ref[:, mid:], gz_ref[:, slow_wide:])
        total = None
        for phase in range(PHASES):
            part = fast[
                phase * fast_part : (phase + 1) * fast_part,
                phase * lanes_fast : (phase + 1) * lanes_fast,
            ]
            total = part if total is None else total + part
        return total

    def space_grad(ha_ref, taps_ref, out_ref, at):
        fast_grads = []
        for tap in range(9):
            value = dot_tn(ha_ref[:, :mid], taps_ref[tap, :, :mid])
            low = at + tap * depth_mid
            out_ref[:, low : low + depth_mid, :] = value.astype(BF16).reshape(
                count, depth_mid, mid
            )
            fast = dot_tn(ha_ref[:, mid:], taps_ref[tap, :, mid:])
            total = None
            for phase in range(PHASES):
                part = lane_block(
                    fast[phase * fast_part : (phase + 1) * fast_part], phase, fast_part
                )
                total = part if total is None else total + part
            fast_grads.append(total)
        if isinstance(out_ref, Store):
            out_ref.send_rows(at, at + 9 * depth_mid)
        return fast_grads

    def put_fast(reduce, space, expand, out_ref, at):
        lane = lax.broadcasted_iota(jnp.int32, reduce[0].shape, 1)

        def beside(parts):
            keep = lane[: parts[0].shape[0]]
            total = None
            for place, part in enumerate(parts):
                part = jnp.where(keep < fast_part, part, 0.0)
                part = pltpu.roll(part, place * fast_part, 1) if place else part
                total = part if total is None else total + part
            return total

        depth = reduce[0].shape[0] // count
        taps = beside(reduce).astype(BF16).reshape(count, depth, lanes_fast)
        out_ref[:, at : at + depth, :] = jnp.concatenate([taps, jnp.zeros_like(taps)], axis=-1)

        def spread(value):
            tiles = value.reshape(count // 2, SUB, lanes_fast)
            return jnp.stack([tiles, pltpu.roll(tiles, SUB // 2, 1)], axis=1).reshape(
                count, SUB, lanes_fast
            )

        first = jnp.concatenate([spread(beside(space[0:4])), spread(beside(space[4:8]))], axis=-1)
        second = jnp.concatenate([spread(beside(space[8:9])), spread(expand)], axis=-1)
        both = jnp.concatenate([first, second], axis=1).astype(BF16)
        out_ref[:, at + depth : at + depth + 2 * SUB, :] = both
        if isinstance(out_ref, Store):
            out_ref.send_rows(at, at + depth + 2 * SUB)

    def space_back_stage(
        g, zb, za, halo, stats_b, parts_b, params_b, stats_a, params_a, g_hbm, at, fast_w
    ):
        def kernel(
            meta_ref,
            inv_ref,
            sums_b_ref,
            g_ref,
            side_ref,
            up_ref,
            down_ref,
            stats_b_ref,
            stats_a_ref,
            zb_ref,
            za_ref,
            params_b_ref,
            params_a_ref,
            fast_ref,
            loads,
            taps_ref,
            g_out,
            sums_out,
        ):
            limit = meta_ref[0]
            coeffs = affine(stats_b_ref, params_b_ref, inv_ref, mid)
            both = [back_rows(sums_b_ref, inv_ref, mid, row) for row in range(2)]

            def back(gradient, value, valid):
                return norm_back(gradient, value, coeffs, both, valid)

            def halo_back(value, scale):
                value = geo.three(value.astype(F32))
                valid = mask_groups(value[..., :small].shape, limit, scale)
                return back(value[..., :small], value[..., small:], valid)

            def edge_back(value):
                value = geo.three(value.astype(F32))
                shape = value[..., :small].shape
                group = lax.broadcasted_iota(jnp.int32, shape, 0) * SUB % EDGE
                group = group + lax.broadcasted_iota(jnp.int32, shape, 1)
                return geo.flat(back(value[..., :small], value[..., small:], group < limit))

            own, zb = geo.three(g_ref[...]), geo.three(zb_ref[...])
            up, down = from_above_and_below(up_ref, down_ref, meta_ref)
            side = side_ref[...].astype(F32)
            edges = jnp.concatenate([up[half_rows:], side, down[half_rows:]], axis=0)

            near_by = Neighbours(
                back(own, zb, mask_groups(own.shape, limit)),
                halo_back(up[:half_rows], 2),
                halo_back(down[:half_rows], 2),
                edge_back(edges),
                meta_ref,
                geo.width,
            )
            slow = fast = None
            for tap in range(9):
                moved = geo.flat(near_by.at(1 - tap // 3, 1 - tap % 3)).astype(BF16)
                taps_ref[tap] = moved
                if tap == 8:
                    taps_ref.send()
                slow_term = dot_nt(moved[:, :mid], loads.get(tap))
                fast_term = dot_nt(moved[:, mid:], fast_ref[tap])
                slow = slow_term if slow is None else slow + slow_term
                fast = fast_term if fast is None else fast + fast_term
            scale, shift, mean, inv = affine(stats_a_ref, params_a_ref, inv_ref, mid)
            za = geo.three(za_ref[...])
            result = geo.three(jnp.concatenate([slow, fast], axis=1)) * slope(za * scale + shift)
            g_out[...] = geo.flat(result)
            masked = jnp.where(mask_groups(result.shape, limit), result, 0.0)
            put_back(sums_out, masked, (za - mean) * inv)

        taps, g, sums, sums_b = run(
            kernel,
            [((9, rows, small), BF16, "hbm"), small_next, stats_small],
            smem=scalars,
            parts=(parts_b,),
            vmem=(g,),
            saved=(*halo, stats_b, stats_a, zb, za, params_b, params_a, fast_w),
            weights=((g_hbm, at, 9, depth_mid),),
        )
        return taps, g, exchange(sums), sums_b

    taps_two, g_a2, parts_a2, sums_b2 = space_back_stage(
        g_b2,
        zb_two,
        za_two,
        halo_back_two,
        stats_b2,
        parts_b2,
        params_two[1],
        stats_a2,
        params_two[0],
        last,
        at_space_two,
        fast_two[3],
    )
    def grads_two_kernel(hb_ref, gz_ref, ha_ref, taps_ref, out_ref, fast_out):
        space = space_grad(ha_ref, taps_ref, out_ref, 0)
        expand_grad(hb_ref, gz_ref, out_ref, 9 * depth_mid)
        for tap in range(9):
            fast_out[tap] = space[tap]
        fast_out[9] = fast_expand_grad(hb_ref, gz_ref)

    rows_space = aligned((9 + blocks) * depth_mid)
    packed_space, fast_space_two = run(
        grads_two_kernel,
        [((count, rows_space, mid), BF16, "rows"), ((10, fast_part, lanes_fast), F32, "hbm")],
        saved=(hb_two, gz_c2, ha_two, taps_two),
    )
    sum_space = lax.psum_scatter(packed_space, TILE, scatter_dimension=0, tiled=False)

    def reduce_gz(meta_ref, inv_ref, g_ref, za_ref, stats_ref, sums_ref, params_ref, steps_ref):
        coeffs = affine(stats_ref, params_ref, inv_ref, mid)
        both = [back_rows(sums_ref, inv_ref, mid, row) for row in range(2)]
        gradient = geo.three(g_ref[...])
        gz = norm_back(
            gradient,
            geo.three(za_ref[...]),
            coeffs,
            both,
            mask_groups(gradient.shape, meta_ref[0]),
        )
        gz = geo.flat(gz)
        steps = [geo.shift(gz, -1).astype(BF16), gz.astype(BF16), geo.shift(gz, 1).astype(BF16)]
        for tap in range(3):
            steps_ref[tap] = steps[tap]
        steps_ref.send()
        return steps

    def reduce_back_two_kernel(
        meta_ref,
        inv_ref,
        sums_ref,
        g_ref,
        stats_ref,
        stats_c_ref,
        za_ref,
        params_ref,
        g_two_ref,
        sum_ref,
        zc_ref,
        short_ref,
        main_ref,
        before_ref,
        after_ref,
        loads,
        steps_ref,
        fast_out,
        g_out,
        sums_out,
    ):
        steps = reduce_gz(
            meta_ref, inv_ref, g_ref, za_ref, stats_ref, sums_ref, params_ref, steps_ref
        )
        slow = None
        for tap in range(3):
            term = dot_nt(steps[tap][:, :mid], loads.get(tap))
            slow = term if slow is None else slow + term
        fast = fast_conv_back(
            [step[:, mid:] for step in steps], main_ref[...], before_ref[...], after_ref[...]
        )
        back = jnp.concatenate([slow, fast], axis=1) + g_two_ref[...].astype(F32)
        back = back * slope(sum_ref[...].astype(F32))
        g_out[...] = back.astype(BF16)
        g_out.send()
        fast_out[...] = back[:, slow_wide:]
        fast_out.send()
        back = geo.three(back)
        masked = jnp.where(mask_groups(back.shape, meta_ref[0]), back, 0.0)
        mean, inv = moments(stats_c_ref, inv_ref, slow_wide, 0, wide)
        put_back(sums_out, masked, (geo.three(zc_ref[...].astype(F32)) - mean) * inv)
        mean, inv = moments(stats_c_ref, inv_ref, slow_wide, wide, wide + slow_wide)
        masked = masked[..., :slow_wide]
        put_back(sums_out, masked, (geo.three(short_ref[...].astype(F32)) - mean) * inv, wide)

    steps_two, g_one_fast, g_one, sums, sums_a2 = run(
        reduce_back_two_kernel,
        [
            ((3, rows, small), BF16, "hbm"),
            ((rows, fast_wide), F32, "hbm"),
            wide_low,
            stats_both,
        ],
        smem=scalars,
        parts=(parts_a2,),
        vmem=(g_a2,),
        saved=(stats_a2, stats_c1, za_two, params_two[0], g_two, sum_one, zc_one, short, *fast_two[:3]),
        weights=((far, at_reduce_two, 3, depth_two),),
    )
    parts_c1 = exchange_widest(sums)

    def expand_back_one_kernel(*refs):
        *body, short_ref, short_params_ref, loads, gz_ref, g_out, sums_out, message, edge, gs_ref = (
            refs
        )
        gradient = expand_back_body(*body, loads, gz_ref, g_out, sums_out, message, edge)
        meta_ref, inv_ref, sums_ref, _, stats_ref = body[:5]
        low, high = wide, wide + slow_wide
        coeffs = affine(stats_ref, short_params_ref, inv_ref, slow_wide, low, high)
        both = [back_rows(sums_ref, inv_ref, slow_wide, row, low, high) for row in range(2)]
        gradient = gradient[..., :slow_wide]
        valid = mask_groups(gradient.shape, meta_ref[0])
        gs = norm_back(gradient, geo.three(short_ref[...].astype(F32)), coeffs, both, valid)
        gs_ref[...] = geo.flat(gs).astype(BF16)

    gz_c1, g_b1, sums, message, edges, gz_short, sums_c1 = run(
        expand_back_one_kernel,
        [((rows, wide), BF16, "hbm"), small_next, stats_small, *message_back]
        + [((rows, slow_wide), BF16, "hbm")],
        smem=scalars,
        parts=(parts_c1,),
        saved=(g_one, stats_c1, stats_b1, zc_one, params_one[2], zb_one, params_one[1], fast_one[4])
        + (short, params_short),
        weights=((far, 0, blocks, depth_mid),),
    )
    parts_b1 = exchange(sums)
    halo_back_one = exchange_halo(message, edges)
    joined_lanes = slow_wide + lat

    def grads_mid_kernel(
        x_ref,
        united_ref,
        gs_ref,
        hb_ref,
        gz_ref,
        low_ref,
        steps_ref,
        fast_ref,
        loads,
        out_ref,
        back_ref,
    ):
        for tap in range(3):
            value = dot_tn(low_ref[:, :slow_wide], steps_ref[tap, :, :mid])
            out_ref[:, tap * depth_two : (tap + 1) * depth_two, :] = value.astype(BF16).reshape(
                count, depth_two, mid
            )
        at = 3 * depth_two
        out_ref.send_rows(0, at)
        reduce = fast_reduce_grad(
            low_ref[:, slow_wide:], [steps_ref[tap, :, mid:] for tap in range(3)]
        )
        put_fast(reduce, [fast_ref[tap] for tap in range(9)], fast_ref[9], out_ref, at)
        at += fast_rows_count
        expand_grad(hb_ref, gz_ref, out_ref, at + blocks * depth_one)
        for block in range(blocks):
            gs = gs_ref[:, block * mid : (block + 1) * mid]
            value = jnp.concatenate([dot_tn(x_ref[...], gs), dot_tn(united_ref[...], gs)], axis=0)
            low = at + block * depth_one
            out_ref[:, low : low + depth_one, :] = value.astype(BF16).reshape(
                count, depth_one, mid
            )
            out_ref.send_rows(low, low + depth_one)
        for block in range(blocks):
            gs = gs_ref[:, block * mid : (block + 1) * mid]
            term = dot_nt(gs, loads.get(block))
            back_ref[...] = term if block == 0 else back_ref[...] + term

    rows_mid = aligned(3 * depth_two + fast_rows_count + blocks * (depth_one + depth_mid))
    packed_mid, short_back = run(
        grads_mid_kernel,
        [((count, rows_mid, mid), BF16, "rows"), ((rows, joined_lanes), F32, "hbm")],
        saved=(slow_x, united, gz_short, hb_one, gz_c1, low_one, steps_two, fast_space_two),
        weights=((far, at_short, blocks, depth_one),),
    )
    sum_mid = lax.psum_scatter(packed_mid, TILE, scatter_dimension=0, tiled=False)

    taps_one, g_a1, parts_a1, sums_b1 = space_back_stage(
        g_b1,
        zb_one,
        za_one,
        halo_back_one,
        stats_b1,
        parts_b1,
        params_one[1],
        stats_a1,
        params_one[0],
        near,
        at_space_one,
        fast_one[3],
    )
    def last_kernel(
        meta_ref,
        inv_ref,
        sums_ref,
        g_ref,
        stats_ref,
        za_ref,
        params_ref,
        g_one_ref,
        short_ref,
        lateral_ref,
        main_ref,
        before_ref,
        after_ref,
        loads,
        steps_ref,
        slow_ref,
        fast_ref,
        united_ref,
    ):
        steps = reduce_gz(
            meta_ref, inv_ref, g_ref, za_ref, stats_ref, sums_ref, params_ref, steps_ref
        )
        joined = short_ref[...]
        for tap in range(3):
            joined = joined + dot_nt(steps[tap][:, :mid], loads.get(tap))
        slow_ref[...] = joined[:, :slow_wide]
        tail = joined[:, slow_wide:]
        now, past = tail.astype(BF16), geo.shift(tail, -1).astype(BF16)
        united_ref[0] = now
        united_ref[1] = past
        lanes = fast_wide // PHASES
        fast = fast_conv_back(
            [step[:, mid:] for step in steps], main_ref[...], before_ref[...], after_ref[...]
        )
        fast = fast + g_one_ref[...]
        front = dot_nt(now, lateral_ref[2:5].reshape(3 * lanes, lat))
        back = dot_nt(past, lateral_ref[0:2].reshape(2 * lanes, lat))
        fast_ref[:, : 2 * lanes] = fast[:, : 2 * lanes] + front[:, : 2 * lanes]
        fast_ref[:, 2 * lanes : 3 * lanes] = (
            fast[:, 2 * lanes : 3 * lanes] + front[:, 2 * lanes :] + back[:, :lanes]
        )
        fast_ref[:, 3 * lanes :] = fast[:, 3 * lanes :] + back[:, lanes:]

    steps_one, grad_slow, grad_fast, united_low, sums_a1 = run(
        last_kernel,
        [
            ((3, rows, small), BF16, "hbm"),
            ((rows, slow_wide), F32, "hbm"),
            ((rows, fast_wide), F32, "hbm"),
            ((2, rows, lat), BF16, "hbm"),
        ],
        smem=scalars,
        parts=(parts_a1,),
        vmem=(g_a1,),
        saved=(stats_a1, za_one, params_one[0], g_one_fast, short_back, lateral, *fast_one[:3]),
        weights=((near, 0, 3, depth_one),),
    )

    def grads_one_kernel(
        meta_ref,
        steps_ref,
        low_ref,
        x_ref,
        united_ref,
        fast_x_ref,
        ha_ref,
        taps_ref,
        hb_ref,
        gz_ref,
        own_ref,
        send_ref,
        out_ref,
        sems,
    ):
        lanes = fast_wide // PHASES
        for tap in range(3):
            step = steps_ref[tap, :, :mid]
            value = jnp.concatenate(
                [dot_tn(x_ref[...], step), dot_tn(united_ref[...], step)], axis=0
            )
            out_ref[:, tap * depth_one : (tap + 1) * depth_one, :] = value.astype(BF16).reshape(
                count, depth_one, mid
            )
        at = 3 * depth_one
        place = (own_ref, send_ref, meta_ref[1], meta_ref[2], sems)
        put_blocks(out_ref, 0, at, *place, 0)
        past = dot_tn(fast_x_ref[:, 2 * lanes :], low_ref[1])
        now = dot_tn(fast_x_ref[:, : 3 * lanes], low_ref[0])
        both = jnp.concatenate([past, now], axis=0).astype(BF16)
        for tap in range(5):
            out_ref[:, at + tap * depth_lat : at + (tap + 1) * depth_lat, :] = both[
                tap * lanes : (tap + 1) * lanes
            ].reshape(count, depth_lat, lat)
        at += 5 * depth_lat
        space = space_grad(ha_ref, taps_ref, out_ref, at)
        at += 9 * depth_mid
        reduce = fast_reduce_grad(
            fast_x_ref[...], [steps_ref[tap, :, mid:] for tap in range(3)]
        )
        put_fast(reduce, space, fast_expand_grad(hb_ref, gz_ref), out_ref, at)

        put_blocks(out_ref, 3 * depth_one, rows_late, *place, 1)
        for low, top, turn in ((0, 3 * depth_one, 0), (3 * depth_one, rows_late, 1)):
            rows_part = pl.ds(low, top - low)
            for block in range(count):
                source, target = out_ref.at[block, rows_part, :], own_ref.at[0, rows_part, :]
                pltpu.make_async_copy(source, target, sems.at[turn, block]).wait()

    def put_blocks(blocks_ref, low, top, own_ref, send_ref, ha, wa, sems, turn):
        rows_part = pl.ds(low, top - low)
        for block in range(count):
            place, col = ha ^ (block // 2), block % 2
            source, sem = blocks_ref.at[block, rows_part, :], sems.at[turn, block]

            @pl.when(wa == col)
            def _():
                pltpu.make_async_copy(source, own_ref.at[place, rows_part, :], sem).start()

            @pl.when(wa != col)
            def _():
                pltpu.make_async_copy(source, send_ref.at[place, rows_part, :], sem).start()

    high = count // 2
    rows_one = 3 * depth_one + 5 * depth_lat + 9 * depth_mid + fast_rows_count
    rows_late = aligned(rows_one)
    blocks_out = ((high, rows_late, mid), BF16, "raw")
    own_blocks, send_blocks = run(
        grads_one_kernel,
        [blocks_out, blocks_out],
        smem=(meta,),
        saved=(steps_one, united_low, slow_x, united, fast_x, ha_one, taps_one, hb_one, gz_c1),
        scratch=(
            pltpu.VMEM((count, rows_late, mid), BF16),
            pltpu.SemaphoreType.DMA((2, count)),
        ),
    )
    side_blocks = lax.ppermute(send_blocks, "wa", xor_pairs(2, 1))

    def chip_kernel(own_ref, side_ref, *out_refs):
        for place in range(high):
            total = own_ref[place].astype(F32) + side_ref[place].astype(F32)
            out_refs[place][...] = total.astype(BF16)
            out_refs[place].send()

    late_out = ((rows_late, mid), BF16, "hbm")
    chip_sums = run(chip_kernel, [late_out] * high, saved=(own_blocks, side_blocks))
    early = jnp.concatenate([sum_space, sum_mid])
    chip_sums, early = lax.optimization_barrier((chip_sums, early))
    late = [chip_sums[0]] + to_partners(chip_sums[1:], "ha")
    four = lax.axis_size("clips") == 4
    parts_early = [lax.psum(early, "clips")]
    quarters = clip_parts(meta, [late], 4 if four else 1)
    if four:
        total_late = add_low(quarters[0], *to_partners(quarters[1:], "clips"))
        parts_late = [total_late] + to_partners([total_late] * 3, "clips")
    else:
        parts_late = [lax.psum(quarters[0], "clips")]

    def finish(*jobs):
        outs_all = []
        for _, groups in jobs:
            for _, shapes in groups:
                for shape in shapes:
                    outs_all += list(shape) if isinstance(shape[0], tuple) else [shape]
        number = sum(len(parts) for parts, _ in jobs)
        deepest = max(sum(rows_group for rows_group, _ in groups) for _, groups in jobs)

        def kernel(meta_ref, *refs):
            ins, outs, total_ref = list(refs[:number]), list(refs[number:-1]), refs[-1]
            for parts, groups in jobs:
                mine, ins = ins[: len(parts)], ins[len(parts) :]
                one_job(meta_ref, mine, outs, total_ref, groups)

        def one_job(meta_ref, ins, outs, total_ref, groups):
            size = len(ins)
            depth = sum(rows_group for rows_group, _ in groups) // size
            base = 0
            for step, ref in enumerate(ins):
                start = pl.multiple_of((meta_ref[4] ^ step) * depth, 16) if size > 1 else 0
                total_ref[pl.ds(start, depth), :] = ref[...].astype(F32)
            for rows_group, shapes in groups:
                at = base
                for shape in shapes:
                    if isinstance(shape[0], tuple):
                        reduce, space, expand = outs.pop(0), outs.pop(0), outs.pop(0)
                        rows_tap, lanes = reduce.shape[1:]
                        for tap in range(3):
                            reduce[tap] = total_ref[
                                at : at + rows_tap, tap * lanes : (tap + 1) * lanes
                            ]
                        few = space.shape[2]
                        for tap in range(9):
                            row = at + rows_tap + tap // SUB * SUB
                            lane = tap % SUB * lanes
                            space[tap // 3, tap % 3] = total_ref[
                                row : row + few, lane : lane + lanes
                            ]
                        row = at + rows_tap + SUB
                        expand[...] = total_ref[row : row + few, expand.shape[1] :]
                        for out in (reduce, space, expand):
                            out.send()
                        at += rows_tap + 2 * SUB
                        continue
                    out = outs.pop(0)
                    if len(shape) == 2 and shape[1] > mid:
                        for block in range(shape[1] // mid):
                            out[:, block * mid : (block + 1) * mid] = total_ref[
                                at : at + shape[0], :
                            ]
                            at += shape[0]
                    else:
                        number = 1
                        for length in shape[:-1]:
                            number *= length
                        out[...] = total_ref[at : at + number, :].reshape(shape)
                        at += number
                    out.send()
                base += rows_group

        return run(
            kernel,
            [(shape, F32, "hbm") for shape in outs_all],
            smem=(meta,),
            saved=[part for parts, _ in jobs for part in parts],
            scratch=(pltpu.VMEM((deepest, mid), F32),),
        )

    shapes_one = tuple(shard.shape for shard in fast_shards_one)
    shapes_two = tuple(shard.shape for shard in fast_shards_two)
    groups_early = [
        (rows_space, [slow_spatial_two.shape, slow_expand_two.shape]),
        (
            rows_mid,
            [slow_reduce_two.shape, shapes_two, slow_shortcut_one.shape, slow_expand_one.shape],
        ),
    ]
    groups_late = [
        (
            rows_late,
            [slow_reduce_one.shape, lateral_weight.shape, slow_spatial_one.shape, shapes_one],
        )
    ]
    finished = finish((parts_early, groups_early), (parts_late, groups_late))
    grad_slow_spatial_two, grad_slow_expand_two, grad_slow_reduce_two = finished[:3]
    fast_two_grads, (grad_slow_shortcut, grad_slow_expand_one) = finished[3:6], finished[6:8]
    grad_slow_reduce_one, grad_lateral, grad_slow_spatial_one, *fast_one_grads = finished[8:]

    def norm_grads(first, second, third):
        slow = [first[:, :mid], second[:, :mid], third[:, :slow_wide]]
        fast = [first[:, mid:], second[:, mid:], third[:, slow_wide:wide]]
        fast = [jnp.sum(part.reshape(2, PHASES, -1), axis=1) for part in fast]
        return slow, fast

    slow_one_p, fast_one_p = norm_grads(sums_a1, sums_b1, sums_c1)
    slow_two_p, fast_two_p = norm_grads(sums_a2, sums_b2, sums_c2)
    grad_slow_norms_one = jnp.concatenate(slow_one_p + [sums_c1[:, wide:]], axis=1)
    grad_slow_norms_two = jnp.concatenate(slow_two_p, axis=1)
    grad_fast_norms_one = jnp.concatenate(fast_one_p, axis=1)
    grad_fast_norms_two = jnp.concatenate(fast_two_p, axis=1)
    return (
        outputs[:, :slow_wide].reshape(slow_input.shape),
        join_phases(outputs[:, slow_wide:], fast_input.shape),
        grad_slow.reshape(slow_input.shape),
        join_phases(grad_fast, fast_input.shape),
        grad_lateral,
        grad_slow_reduce_one,
        grad_slow_spatial_one,
        grad_slow_expand_one,
        grad_slow_shortcut,
        *fast_one_grads,
        grad_slow_reduce_two,
        grad_slow_spatial_two,
        grad_slow_expand_two,
        *fast_two_grads,
        grad_slow_norms_one,
        grad_fast_norms_one,
        grad_slow_norms_two,
        grad_fast_norms_two,
    )


def solution(mesh):
    in_specs = (
        P("clips", None, "ha", "wa", None),
        P("clips", None, "ha", "wa", None),
        P("clips", None, "ha", "wa", None),
        P("clips", None, "ha", "wa", None),
        P("clips"),
        P(None, ("ha", "wa"), None),
        P(None, ("ha", "wa"), None),
        P(None, None, ("ha", "wa"), None),
        P(("ha", "wa"), None),
        P(("ha", "wa"), None),
        P(None, ("ha", "wa"), None),
        P(None, None, ("ha", "wa"), None),
        P(("ha", "wa"), None),
        P(None, ("ha", "wa"), None),
        P(None, None, ("ha", "wa"), None),
        P(("ha", "wa"), None),
        P(None, ("ha", "wa"), None),
        P(None, None, ("ha", "wa"), None),
        P(("ha", "wa"), None),
        P(),
        P(),
        P(),
        P(),
    )
    out_specs = (
        P("clips", None, "ha", "wa", None),
        P("clips", None, "ha", "wa", None),
        P("clips", None, "ha", "wa", None),
        P("clips", None, "ha", "wa", None),
        P(None, ("ha", "wa"), None),
        P(None, ("ha", "wa"), None),
        P(None, None, ("ha", "wa"), None),
        P(("ha", "wa"), None),
        P(("ha", "wa"), None),
        P(None, ("ha", "wa"), None),
        P(None, None, ("ha", "wa"), None),
        P(("ha", "wa"), None),
        P(None, ("ha", "wa"), None),
        P(None, None, ("ha", "wa"), None),
        P(("ha", "wa"), None),
        P(None, ("ha", "wa"), None),
        P(None, None, ("ha", "wa"), None),
        P(("ha", "wa"), None),
        P(),
        P(),
        P(),
        P(),
    )
    return jax.shard_map(
        on_device, mesh=mesh, in_specs=in_specs, out_specs=out_specs, check_vma=False
    )
```

profile of v0, /device:TPU:0, one launch (start us, length us, event | category | flops | bytes accessed | tf_op | source)
XLA Modules:
  0.0 393.0 jit_solution(9257252220852880991)
XLA Ops:
  18.9 12.3 %all-gather = bf16[2688,128]{1,0:T(8,128)(2,1)S(1)} all-gather(bf16[336,128]{1,0:T(8,128)(2,1)S(1)} %fusion.5), channel_id=2, replica_groups=mesh['clips'=4,'ha'=4,'wa'=2] {'ha','wa'}, dimensions={0}, use_global_device_ids=true | all-gather | bytes 774144 | tf_op jit(solution)/shard_map/all_gather | solution.py:524
  38.0 9.8 %all-gather.8.cloned.1.call-done = bf16[6144,256]{1,0:T(8,128)(2,1)} async-done(((bf16[768,256]{1,0:T(8,128)(2,1)}), bf16[6144,256]{1,0:T(8,128)(2,1)}) %all-gather.8.cloned.1.call-update) | async-done | bytes 3145744 | tf_op jit(solution)/shard_map/all_gather | solution.py:524
  59.4 5.7 %collective-permute-done.4.refs_5_ = bf16[128,384]{1,0:T(8,128)(2,1)S(1)} collective-permute-done((bf16[128,384]{1,0:T(8,128)(2,1)S(1)}, bf16[128,384]{1,0:T(8,128)(2,1)S(1)}, u32[]{:S(2)}, u32[]{:S(2)}) %collective-permute-start.4) | collective-permute-done | bytes 98336 | tf_op jit(solution)/shard_map/ppermute | solution.py:452
  68.7 16.8 %all_to_all.60.refs_2_ = f32[32,2,384]{2,1,0:T(2,128)S(1)} all-to-all(f32[32,2,384]{2,1,0:T(2,128)S(1)} %get-tuple-element.150), channel_id=1, replica_groups=mesh['clips'=4,'ha'=4,'wa'=2] {'clips','ha','wa'}, dimensions={0} | all-to-all | bytes 196608 | tf_op jit(solution)/shard_map/all_to_all | solution.py:435
  85.5 9.0 %all-gather.10.cloned.1.call-done = bf16[9216,256]{1,0:T(8,128)(2,1)} async-done(((bf16[1152,256]{1,0:T(8,128)(2,1)}), bf16[9216,256]{1,0:T(8,128)(2,1)}) %all-gather.10.cloned.1.call-update) | async-done | bytes 4718608 | tf_op jit(solution)/shard_map/all_gather | solution.py:524
  94.5 5.3 %shard_map.394 = (bf16[192,384]{1,0:T(8,128)(2,1)S(1)}, bf16[192,1536]{1,0:T(8,128)(2,1)}, bf16[192,1024]{1,0:T(8,128)(2,1)}, f32[2,2560]{1,0:T(2,128)S(1)}, f32[2,384]{1,0:T(2,128)S(1)}) custom-call(s32[5]{0:T(128)S(1)} %stack.61.refs_0_, f32[2]{0:T(128)S(1)} %pad_maximum_fusion.21.refs_1_, f32[32,2,384]{2,1,0:T(2,128)S(1)} %all_to_all.60.refs_2_, ...), custom_call_target="tpu_custom_call" | custom-call | flops 2000000000 | bytes 16000000 | tf_op jit(solution)/shard_map/pallas_call | solution.py:202
  109.4 9.2 %all_to_all.61.refs_2_ = f32[8,2,2560]{2,1,0:T(2,128)S(1)} all-to-all(f32[8,2,2560]{2,1,0:T(2,128)S(1)} %broadcast_in_dim.7), channel_id=1, replica_groups=mesh['clips'=4,'ha'=4,'wa'=2] {'ha','wa'}, dimensions={0} | all-to-all | bytes 327680 | tf_op jit(solution)/shard_map/all_to_all | solution.py:442
  136.7 13.7 %all_to_all.62.refs_2_ = f32[32,2,384]{2,1,0:T(2,128)S(1)} all-to-all(f32[32,2,384]{2,1,0:T(2,128)S(1)} %get-tuple-element.168), channel_id=1, replica_groups=mesh['clips'=4,'ha'=4,'wa'=2] {'clips','ha','wa'}, dimensions={0} | all-to-all | bytes 196608 | tf_op jit(solution)/shard_map/all_to_all | solution.py:435
  158.6 12.0 %all-to-all-done.5.refs_2_ = f32[32,2,1536]{2,1,0:T(2,128)S(1)} async-done(((f32[32,2,1536]{2,1,0:T(2,128)}), f32[32,2,1536]{2,1,0:T(2,128)S(1)}, u32[]{:S(2)}, u32[]{:S(2)}) %all-to-all-start.5) | async-done | bytes 393248 | tf_op jit(solution)/shard_map/all_to_all | solution.py:435
  174.2 15.6 %all_to_all.63.refs_2_ = f32[32,2,1536]{2,1,0:T(2,128)} all-to-all(f32[32,2,1536]{2,1,0:T(2,128)S(1)} %get-tuple-element.177), channel_id=1, replica_groups=mesh['clips'=4,'ha'=4,'wa'=2] {'clips','ha','wa'}, dimensions={0} | all-to-all | bytes 786432 | tf_op jit(solution)/shard_map/all_to_all | solution.py:435
  196.5 12.9 %all_to_all.64.refs_2_ = f32[32,2,384]{2,1,0:T(2,128)S(1)} all-to-all(f32[32,2,384]{2,1,0:T(2,128)S(1)} %get-tuple-element.181), channel_id=1, replica_groups=mesh['clips'=4,'ha'=4,'wa'=2] {'clips','ha','wa'}, dimensions={0} | all-to-all | bytes 196608 | tf_op jit(solution)/shard_map/all_to_all | solution.py:435
  209.4 5.6 %shard_map.400 = (bf16[9,192,384]{2,1,0:T(8,128)(2,1)}, f32[192,384]{1,0:T(8,128)}, f32[32,2,384]{2,1,0:T(2,128)S(1)}, f32[2,384]{1,0:T(2,128)S(1)}) custom-call(s32[5]{0:T(128)S(1)} %stack.61.refs_0_, f32[2]{0:T(128)S(1)} %pad_maximum_fusion.21.refs_1_, f32[32,2,384]{2,1,0:T(2,128)S(1)} %all_to_all.64.refs_2_, f32[192,384]{1,0:T(8,128)} %copy-done.13, ...), custom_call_target="tpu_custom_call" | custom-call | flops 2000000000 | bytes 16000000 | tf_op jit(solution)/shard_map/pallas_call | solution.py:202
  218.7 9.6 %all_to_all.65.refs_2_ = f32[32,2,384]{2,1,0:T(2,128)S(1)} all-to-all(f32[32,2,384]{2,1,0:T(2,128)S(1)} %get-tuple-element.186), channel_id=1, replica_groups=mesh['clips'=4,'ha'=4,'wa'=2] {'clips','ha','wa'}, dimensions={0} | all-to-all | bytes 196608 | tf_op jit(solution)/shard_map/all_to_all | solution.py:435
  240.8 8.3 %all_to_all.66.refs_2_ = f32[8,2,2560]{2,1,0:T(2,128)S(1)} all-to-all(f32[8,2,2560]{2,1,0:T(2,128)S(1)} %broadcast_in_dim.8), channel_id=1, replica_groups=mesh['clips'=4,'ha'=4,'wa'=2] {'ha','wa'}, dimensions={0} | all-to-all | bytes 327680 | tf_op jit(solution)/shard_map/all_to_all | solution.py:442
  249.1 5.5 %shard_map.402 = (bf16[192,1536]{1,0:T(8,128)(2,1)}, f32[192,384]{1,0:T(8,128)S(1)}, f32[32,2,384]{2,1,0:T(2,128)S(1)}, bf16[192,768]{1,0:T(8,128)(2,1)}, bf16[6...) custom-call(s32[5]{0:T(128)S(1)} %stack.61.refs_0_, f32[2]{0:T(128)S(1)} %pad_maximum_fusion.21.refs_1_, ...), custom_call_target="tpu_custom_call" | custom-call | flops 2000000000 | bytes 16000000 | tf_op jit(solution)/shard_map/pallas_call | solution.py:202
  254.7 6.4 %shard_map.405 = (bf16[8,1216,256]{2,1,0:T(8,128)(2,1)}, f32[192,1280]{1,0:T(8,128)}) custom-call(bf16[192,1024]{1,0:T(8,128)(2,1)S(1)} %copy-done, bf16[192,256]{1,0:T(8,128)(2,1)S(1)} %get-tuple-element.142.refs_2_.refs_7_.refs_1_.refs_4_, bf16[192,1024]{1,0:T(8,128)(2,1)} %get-tuple-element.200.refs_2_, ...), custom_call_target="tpu_custom_call" | custom-call | flops 2000000000 | bytes 16000000 | tf_op jit(solution)/shard_map/pallas_call | solution.py:202
  263.9 14.4 %all_to_all.67.refs_2_ = f32[32,2,384]{2,1,0:T(2,128)S(1)} all-to-all(f32[32,2,384]{2,1,0:T(2,128)S(1)} %get-tuple-element.192), channel_id=1, replica_groups=mesh['clips'=4,'ha'=4,'wa'=2] {'clips','ha','wa'}, dimensions={0} | all-to-all | bytes 196608 | tf_op jit(solution)/shard_map/all_to_all | solution.py:435
  278.2 5.6 %shard_map.403 = (bf16[9,192,384]{2,1,0:T(8,128)(2,1)}, f32[192,384]{1,0:T(8,128)}, f32[32,2,384]{2,1,0:T(2,128)S(1)}, f32[2,384]{1,0:T(2,128)S(1)}) custom-call(s32[5]{0:T(128)S(1)} %stack.61.refs_0_, f32[2]{0:T(128)S(1)} %pad_maximum_fusion.21.refs_1_, f32[32,2,384]{2,1,0:T(2,128)S(1)} %all_to_all.67.refs_2_, f32[192,384]{1,0:T(8,128)} %copy-done.8, ...), custom_call_target="tpu_custom_call" | custom-call | flops 2000000000 | bytes 16000000 | tf_op jit(solution)/shard_map/pallas_call | solution.py:202
  283.8 9.6 %all_to_all.68.refs_2_ = f32[32,2,384]{2,1,0:T(2,128)S(1)} all-to-all(f32[32,2,384]{2,1,0:T(2,128)S(1)} %get-tuple-element.197), channel_id=1, replica_groups=mesh['clips'=4,'ha'=4,'wa'=2] {'clips','ha','wa'}, dimensions={0} | all-to-all | bytes 196608 | tf_op jit(solution)/shard_map/all_to_all | solution.py:435
  324.9 6.6 %collective-permute-done.22.refs_2_ = bf16[896,256]{1,0:T(8,128)(2,1)} collective-permute-done((bf16[896,256]{1,0:T(8,128)(2,1)S(1)}, bf16[896,256]{1,0:T(8,128)(2,1)}, u32[]{:S(2)}, u32[]{:S(2)}) %collective-permute-start.22) | collective-permute-done | bytes 458784 | tf_op jit(solution)/shard_map/ppermute | solution.py:609
  331.6 9.8 %collective-permute-done.23.refs_3_ = bf16[896,256]{1,0:T(8,128)(2,1)} collective-permute-done((bf16[896,256]{1,0:T(8,128)(2,1)S(1)}, bf16[896,256]{1,0:T(8,128)(2,1)}, u32[]{:S(2)}, u32[]{:S(2)}) %collective-permute-start.23) | collective-permute-done | bytes 458784 | tf_op jit(solution)/shard_map/ppermute | solution.py:609
  350.0 6.1 %collective-permute-done.26 = bf16[224,256]{1,0:T(8,128)(2,1)S(1)} collective-permute-done((bf16[224,256]{1,0:T(8,128)(2,1)S(1)}, bf16[224,256]{1,0:T(8,128)(2,1)S(1)}, u32[]{:S(2)}, u32[]{:S(2)}) %collective-permute-start.26) | collective-permute-done | bytes 114720 | tf_op jit(solution)/shard_map/ppermute | solution.py:609
  367.8 8.4 %collective-permute-done.29.refs_4_ = bf16[224,256]{1,0:T(8,128)(2,1)S(1)} collective-permute-done((bf16[224,256]{1,0:T(8,128)(2,1)S(1)}, bf16[224,256]{1,0:T(8,128)(2,1)S(1)}, u32[]{:S(2)}, u32[]{:S(2)}) %collective-permute-start.29) | collective-permute-done | bytes 114720 | tf_op jit(solution)/shard_map/ppermute | solution.py:609
  376.2 5.8 %all-reduce.4.cloned.1.call-done.refs_1_ = bf16[1664,256]{1,0:T(8,128)(2,1)} async-done(((bf16[1664,256]{1,0:T(8,128)(2,1)}), bf16[1664,256]{1,0:T(8,128)(2,1)}) %all-reduce.4.cloned.1.call-update) | async-done | bytes 851984 | tf_op jit(solution)/shard_map/psum | solution.py:1617
  (255 shorter events, 153.0 us)
Async XLA Ops:
  7.2 40.6 %all-gather.8.cloned.1.call-start = ((), (), s32[]{:S(2)}) async-start(), calls=%async_computation.17 | async-start | bytes 3538944 | tf_op jit(solution)/shard_map/all_gather | solution.py:524
  9.2 85.3 %all-gather.10.cloned.1.call-start = ((), (), s32[]{:S(2)}) async-start(), calls=%async_computation.18 | async-start | bytes 5308416 | tf_op jit(solution)/shard_map/all_gather | solution.py:524
  11.5 116.2 %all-gather.12.cloned.1.call-start = ((), (), s32[]{:S(2)}) async-start(), calls=%async_computation.19 | async-start | bytes 1916928 | tf_op jit(solution)/shard_map/all_gather | solution.py:524
  12.2 25.6 %collective-permute-start = (f32[1,128]{1,0:T(1,128)S(1)}, f32[1,128]{1,0:T(1,128)S(1)}, u32[]{:S(2)}, u32[]{:S(2)}) collective-permute-start(f32[1,128]{1,0:T(1,128)S(1)} %broadcast_in_dim.6), channel_id=1, source_target_pairs={{0,16},{8,24},{16,0},{24,8},{1,17},{9,25},{17,1},{25,9},{2,18},{10... | collective-permute-start | bytes 1544 | tf_op jit(solution)/shard_map/ppermute | solution.py:413
  16.3 21.5 %collective-permute-start.1 = (f32[1,128]{1,0:T(1,128)S(1)}, f32[1,128]{1,0:T(1,128)S(1)}, u32[]{:S(2)}, u32[]{:S(2)}) collective-permute-start(f32[1,128]{1,0:T(1,128)S(1)} %broadcast_in_dim.6), channel_id=1, source_target_pairs={{0,8},{8,0},{16,24},{24,16},{1,9},{9,1},{17,25},{25,17},{2,10},{10... | collective-permute-start | bytes 1544 | tf_op jit(solution)/shard_map/ppermute | solution.py:413
  17.9 19.9 %collective-permute-start.2 = (f32[1,128]{1,0:T(1,128)S(1)}, f32[1,128]{1,0:T(1,128)S(1)}, u32[]{:S(2)}, u32[]{:S(2)}) collective-permute-start(f32[1,128]{1,0:T(1,128)S(1)} %broadcast_in_dim.6), channel_id=1, source_target_pairs={{0,24},{8,16},{16,8},{24,0},{1,25},{9,17},{17,9},{25,1},{2,26},{10... | collective-permute-start | bytes 1544 | tf_op jit(solution)/shard_map/ppermute | solution.py:413
  52.1 12.9 %all-to-all-start = ((f32[32,2,384]{2,1,0:T(2,128)}), f32[32,2,384]{2,1,0:T(2,128)S(1)}, u32[]{:S(2)}, u32[]{:S(2)}) async-start(f32[32,2,384]{2,1,0:T(2,128)} %get-tuple-element.144), calls=%async_computation | async-start | bytes 196608 | tf_op jit(solution)/shard_map/all_to_all | solution.py:435
  122.6 10.4 %all-to-all-start.3 = ((f32[32,2,384]{2,1,0:T(2,128)}), f32[32,2,384]{2,1,0:T(2,128)S(1)}, u32[]{:S(2)}, u32[]{:S(2)}) async-start(f32[32,2,384]{2,1,0:T(2,128)} %get-tuple-element.162), calls=%async_computation.3 | async-start | bytes 196608 | tf_op jit(solution)/shard_map/all_to_all | solution.py:435
  154.7 15.9 %all-to-all-start.5 = ((f32[32,2,1536]{2,1,0:T(2,128)}), f32[32,2,1536]{2,1,0:T(2,128)S(1)}, u32[]{:S(2)}, u32[]{:S(2)}) async-start(f32[32,2,1536]{2,1,0:T(2,128)} %get-tuple-element.172), calls=%async_computation.5 | async-start | bytes 786432 | tf_op jit(solution)/shard_map/all_to_all | solution.py:435
  157.5 156.5 %reduce-scatter.3.cloned.1.call-start = ((), (), s32[]{:S(2)}) async-start(), calls=%async_computation.14 | async-start | bytes 2064384 | tf_op jit(solution)/shard_map/reduce_scatter | solution.py:1294
  195.2 14.3 %collective-permute-start.13 = (bf16[128,768]{1,0:T(8,128)(2,1)S(1)}, bf16[128,768]{1,0:T(8,128)(2,1)S(1)}, u32[]{:S(2)}, u32[]{:S(2)}) collective-permute-start(bf16[128,768]{1,0:T(8,128)(2,1)S(1)} %get-tuple-element.257), channel_id=1, source_target_pairs={{0,2},{2,0},{4,6},{6,4},{1,3},{3,1},{5,7},{7,5},{8,10},{10,8},{12,... | collective-permute-start | bytes 589832 | tf_op jit(solution)/shard_map/ppermute | solution.py:452
  195.8 13.6 %collective-permute-start.14 = (bf16[128,768]{1,0:T(8,128)(2,1)S(1)}, bf16[128,768]{1,0:T(8,128)(2,1)S(1)}, u32[]{:S(2)}, u32[]{:S(2)}) collective-permute-start(bf16[128,768]{1,0:T(8,128)(2,1)S(1)} %get-tuple-element.256), channel_id=1, source_target_pairs={{2,4},{4,2},{3,5},{5,3},{10,12},{12,10},{11,13},{13,11},{18,20},{2... | collective-permute-start | bytes 589832 | tf_op jit(solution)/shard_map/ppermute | solution.py:455
  218.7 97.3 %reduce-scatter.5.cloned.1.call-start = ((), (), s32[]{:S(2)}) async-start(), calls=%async_computation.15 | async-start | bytes 5603328 | tf_op jit(solution)/shard_map/reduce_scatter | solution.py:1450
  261.1 120.9 %all-reduce.4.cloned.1.call-start = ((), (), s32[]{:S(2)}) async-start(), calls=%async_computation.16 | async-start | bytes 1703936 | tf_op jit(solution)/shard_map/psum | solution.py:1617
  262.6 15.7 %collective-permute-start.19 = (bf16[128,768]{1,0:T(8,128)(2,1)S(1)}, bf16[128,768]{1,0:T(8,128)(2,1)S(1)}, u32[]{:S(2)}, u32[]{:S(2)}) collective-permute-start(bf16[128,768]{1,0:T(8,128)(2,1)S(1)} %get-tuple-element.255), channel_id=1, source_target_pairs={{0,2},{2,0},{4,6},{6,4},{1,3},{3,1},{5,7},{7,5},{8,10},{10,8},{12,... | collective-permute-start | bytes 589832 | tf_op jit(solution)/shard_map/ppermute | solution.py:452
  263.2 15.0 %collective-permute-start.20 = (bf16[128,768]{1,0:T(8,128)(2,1)S(1)}, bf16[128,768]{1,0:T(8,128)(2,1)S(1)}, u32[]{:S(2)}, u32[]{:S(2)}) collective-permute-start(bf16[128,768]{1,0:T(8,128)(2,1)S(1)} %get-tuple-element.254), channel_id=1, source_target_pairs={{2,4},{4,2},{3,5},{5,3},{10,12},{12,10},{11,13},{13,11},{18,20},{2... | collective-permute-start | bytes 589832 | tf_op jit(solution)/shard_map/ppermute | solution.py:455
  318.1 13.5 %collective-permute-start.22 = (bf16[896,256]{1,0:T(8,128)(2,1)S(1)}, bf16[896,256]{1,0:T(8,128)(2,1)}, u32[]{:S(2)}, u32[]{:S(2)}) collective-permute-start(bf16[896,256]{1,0:T(8,128)(2,1)S(1)} %get-tuple-element.227), channel_id=1, source_target_pairs={{0,2},{2,0},{4,6},{6,4},{1,3},{3,1},{5,7},{7,5},{8,10},{10,8},{12,... | collective-permute-start | bytes 1376264 | tf_op jit(solution)/shard_map/ppermute | solution.py:609
  319.5 21.9 %collective-permute-start.23 = (bf16[896,256]{1,0:T(8,128)(2,1)S(1)}, bf16[896,256]{1,0:T(8,128)(2,1)}, u32[]{:S(2)}, u32[]{:S(2)}) collective-permute-start(bf16[896,256]{1,0:T(8,128)(2,1)S(1)} %copy-done.35), channel_id=1, source_target_pairs={{0,4},{2,6},{4,0},{6,2},{1,5},{3,7},{5,1},{7,3},{8,12},{10,14},{12... | collective-permute-start | bytes 1376264 | tf_op jit(solution)/shard_map/ppermute | solution.py:609
  320.1 21.3 %collective-permute-start.24 = (bf16[896,256]{1,0:T(8,128)(2,1)S(1)}, bf16[896,256]{1,0:T(8,128)(2,1)}, u32[]{:S(2)}, u32[]{:S(2)}) collective-permute-start(bf16[896,256]{1,0:T(8,128)(2,1)S(1)} %copy-done.34), channel_id=1, source_target_pairs={{0,6},{2,4},{4,2},{6,0},{1,7},{3,5},{5,3},{7,1},{8,14},{10,12},{12... | collective-permute-start | bytes 1376264 | tf_op jit(solution)/shard_map/ppermute | solution.py:609
  345.3 10.8 %collective-permute-start.26 = (bf16[224,256]{1,0:T(8,128)(2,1)S(1)}, bf16[224,256]{1,0:T(8,128)(2,1)S(1)}, u32[]{:S(2)}, u32[]{:S(2)}) collective-permute-start(bf16[224,256]{1,0:T(8,128)(2,1)S(1)} %get-tuple-element.232), channel_id=1, source_target_pairs={{0,16},{8,24},{16,0},{24,8},{1,17},{9,25},{17,1},{25,9},{2,18},{10... | collective-permute-start | bytes 344072 | tf_op jit(solution)/shard_map/ppermute | solution.py:609
  347.7 8.4 %collective-permute-start.27 = (bf16[224,256]{1,0:T(8,128)(2,1)S(1)}, bf16[224,256]{1,0:T(8,128)(2,1)S(1)}, u32[]{:S(2)}, u32[]{:S(2)}) collective-permute-start(bf16[224,256]{1,0:T(8,128)(2,1)S(1)} %get-tuple-element.233), channel_id=1, source_target_pairs={{0,24},{8,16},{16,8},{24,0},{1,25},{9,17},{17,9},{25,1},{2,26},{10... | collective-permute-start | bytes 344072 | tf_op jit(solution)/shard_map/ppermute | solution.py:609
  356.2 11.6 %collective-permute-start.28 = (bf16[224,256]{1,0:T(8,128)(2,1)S(1)}, bf16[224,256]{1,0:T(8,128)(2,1)S(1)}, u32[]{:S(2)}, u32[]{:S(2)}) collective-permute-start(bf16[224,256]{1,0:T(8,128)(2,1)S(1)} %add_convert_fusion.refs_2_), channel_id=1, source_target_pairs={{0,8},{8,0},{16,24},{24,16},{1,9},{9,1},{17,25},{25,17},{2,10},{10... | collective-permute-start | bytes 344072 | tf_op jit(solution)/shard_map/ppermute | solution.py:609
  358.0 18.1 %collective-permute-start.29 = (bf16[224,256]{1,0:T(8,128)(2,1)S(1)}, bf16[224,256]{1,0:T(8,128)(2,1)S(1)}, u32[]{:S(2)}, u32[]{:S(2)}) collective-permute-start(bf16[224,256]{1,0:T(8,128)(2,1)S(1)} %add_convert_fusion.refs_2_), channel_id=1, source_target_pairs={{0,16},{8,24},{16,0},{24,8},{1,17},{9,25},{17,1},{25,9},{2,18},{10... | collective-permute-start | bytes 344072 | tf_op jit(solution)/shard_map/ppermute | solution.py:609
  359.7 16.5 %collective-permute-start.30 = (bf16[224,256]{1,0:T(8,128)(2,1)S(1)}, bf16[224,256]{1,0:T(8,128)(2,1)S(1)}, u32[]{:S(2)}, u32[]{:S(2)}) collective-permute-start(bf16[224,256]{1,0:T(8,128)(2,1)S(1)} %add_convert_fusion.refs_2_), channel_id=1, source_target_pairs={{0,24},{8,16},{16,8},{24,0},{1,25},{9,17},{17,9},{25,1},{2,26},{10... | collective-permute-start | bytes 344072 | tf_op jit(solution)/shard_map/ppermute | solution.py:609
  (52 other events, 342.3 us)
Sparse Core Ops, SparseCore 0:
  10.5 37.2 all-gather.7
  50.3 44.1 all-gather.9
  96.4 26.8 all-gather.11
  218.8 36.7 reduce-scatter.2
  261.2 54.7 reduce-scatter.4
  325.1 56.8 all-reduce.3
where the time goes:
time: 394 us; the launch traced here: 393 us
  blocking collectives  122 us (31%)
  waiting for transfers between devices  99.3 us (25%)
  Pallas kernels  86.8 us (22%)
  starting transfers between devices  45.7 us (12%)
  between operations  16 us (4%)
  local copies, waits for them, and re-layouts  13.1 us (3%)
  other arithmetic  9.5 us (2%)
    all_to_all x7, blocking collectives, exchange(): return lax.all_to_all(copies, AXES, 0, 0)  92.7 us
    pallas_call x21, Pallas kernels, run(): pl.pallas_call(kernel, out_shape=[jax.ShapeDtypeStruct(shape, dtype) for...  86.8 us
    ppermute x9, waiting for transfers between devices, to_partners(): lax.ppermute(piece, axis, xor_pairs(size, step + 1))  35.8 us
    all_gather x3, waiting for transfers between devices, gather_pack(): return lax.all_gather(jnp.concatenate(parts, axis=0), TILE, axis=0)  18.9 us
    all_to_all x2, blocking collectives, exchange_widest(): lax.all_to_all(jnp.broadcast_to(sums[None], (count,) + sums.shape), TILE,...  17.5 us
    ppermute x9, starting transfers between devices, direct_sum(): lax.ppermute(value, axis, xor_pairs(size, step * times))  14.6 us
    all_to_all x3, waiting for transfers between devices, exchange(): return lax.all_to_all(copies, AXES, 0, 0)  14.1 us
    ppermute x9, starting transfers between devices, to_partners(): lax.ppermute(piece, axis, xor_pairs(size, step + 1))  12.8 us
  transfers between devices with their start and end apart: 40, of which 22 were waited for; matrix products, arithmetic and copies ran while one was open for 4% of the time, Pallas kernels for 15%

commit v1 on v0

--- a/solution.py
+++ b/solution.py
@@ -254,15 +254,11 @@
 def fold(value, slow):
     fast = value[:, slow:]
     lanes = fast.shape[-1]
-    part = lanes // PHASES
-    if part % 128 == 0:
-        total = fast[:, :part]
-        for phase in range(1, PHASES):
-            total = total + fast[:, phase * part : (phase + 1) * part]
-        return jnp.concatenate([value[:, :slow]] + [total] * PHASES, axis=1)
+    if lanes * PHASES <= slow:
+        return jnp.concatenate([value[:, :slow]] + [fast] * PHASES, axis=1)
     total = fast
     for phase in range(1, PHASES):
-        total = total + pltpu.roll(fast, phase * part, 1)
+        total = total + pltpu.roll(fast, phase * (lanes // PHASES), 1)
     return jnp.concatenate([value[:, :slow], total], axis=1)
 
 
@@ -276,7 +272,7 @@
     total, square = rep(stats, 0, low, high), rep(stats, 1, low, high)
     if slow < high - low:
         total, square = fold(total, slow), fold(square, slow)
-    inv_n = lane_counts(inv_ref, high - low, slow)
+    inv_n = lane_counts(inv_ref, total.shape[1], slow)
     mean = total * inv_n
     return mean, lax.rsqrt(square * inv_n - mean * mean + epsilon)
 
@@ -293,7 +289,7 @@
     total = rep(sums, row, low, high)
     if slow < high - low:
         total = fold(total, slow)
-    return total * lane_counts(inv_ref, high - low, slow)
+    return total * lane_counts(inv_ref, total.shape[1], slow)
 
 
 def silu(value):
@@ -305,19 +301,25 @@
     return sigma * (1.0 + value * (1.0 - sigma))
 
 
-def put_stats(ref, first, second, low=0):
-    lanes = first.shape[-1]
-    ref[0:1, low : low + lanes] = jnp.sum(jnp.sum(first, axis=0), axis=0, keepdims=True)
-    ref[1:2, low : low + lanes] = jnp.sum(jnp.sum(second, axis=0), axis=0, keepdims=True)
-
-
-def put_back(ref, gradient, normal, low=0):
-    put_stats(ref, gradient * normal, gradient, low)
-
-
-def put_forward(ref, value, limit, low=0):
+def put_stats(ref, first, second, low=0, slow=None):
+    for row, value in enumerate((first, second)):
+        total = jnp.sum(jnp.sum(value, axis=0), axis=0, keepdims=True)
+        if slow is not None:
+            part = (total.shape[1] - slow) // PHASES
+            fast = total[:, slow : slow + part]
+            for phase in range(1, PHASES):
+                fast = fast + total[:, slow + phase * part : slow + (phase + 1) * part]
+            total = jnp.concatenate([total[:, :slow], fast], axis=1)
+        ref[row : row + 1, low : low + total.shape[1]] = total
+
+
+def put_back(ref, gradient, normal, low=0, slow=None):
+    put_stats(ref, gradient * normal, gradient, low, slow)
+
+
+def put_forward(ref, value, limit, low=0, slow=None):
     masked = jnp.where(mask_groups(value.shape, limit), value, 0.0)
-    put_stats(ref, masked, masked * value, low)
+    put_stats(ref, masked, masked * value, low, slow)
 
 
 EDGE = 32
@@ -683,6 +685,7 @@
     slow_wide = slow_input.shape[-1]
     fast_wide = PHASES * fast_input.shape[-1]
     wide = slow_wide + fast_wide
+    packed = slow_wide + fast_wide // PHASES
     mid = slow_reduce_one.shape[-1]
     fast_part = fast_reduce_one.shape[-1]
     fast_mid = PHASES * fast_part
@@ -746,8 +749,8 @@
     )
     message_out = [((rows, small), BF16, "hbm"), ((2 * EDGE, small), BF16, "hbm")]
     stats_small = ((spread, 2, small), F32, "spread")
-    stats_wide = ((spread, 2, wide), F32, "spread")
-    stats_both = ((2, wide + slow_wide), F32, "vmem")
+    stats_wide = ((spread, 2, packed), F32, "spread")
+    stats_both = ((2, packed + slow_wide), F32, "vmem")
     small_out = ((rows, small), F32, "hbm")
     wide_out = ((rows, wide), F32, "hbm")
     small_both = ((rows, small), F32, "both")
@@ -886,12 +889,12 @@
         expand_body(
             inv_ref, stats_ref, zb_ref, params_ref, fast_ref, hidden_ref, low_ref, zc_ref, loads
         )
-        put_forward(out_stats, geo.three(zc_ref[...]), meta_ref[0])
+        put_forward(out_stats, geo.three(zc_ref[...]), meta_ref[0], 0, slow_wide)
         for block in range(blocks):
             weight = shorts.get(block)
             value = dot(x_ref[...], weight[:slow_wide]) + dot(united_ref[...], weight[slow_wide:])
             short_ref[:, block * mid : (block + 1) * mid] = value
-            put_forward(out_stats, geo.three(value), meta_ref[0], wide + block * mid)
+            put_forward(out_stats, geo.three(value), meta_ref[0], packed + block * mid)
         short_low_ref[...] = short_ref[...].astype(BF16)
         short_low_ref.send()
 
@@ -932,9 +935,9 @@
         message_ref,
         edge_ref,
     ):
-        scale, shift, _, _ = affine(stats_ref, params_ref, inv_ref, slow_wide, 0, wide)
+        scale, shift, _, _ = affine(stats_ref, params_ref, inv_ref, slow_wide, 0, packed)
         scale_s, shift_s, _, _ = affine(
-            stats_ref, short_params_ref, inv_ref, slow_wide, wide, wide + slow_wide
+            stats_ref, short_params_ref, inv_ref, slow_wide, packed, packed + slow_wide
         )
         normed = geo.three(zc_ref[...].astype(F32)) * scale + shift
         slow = normed[..., :slow_wide] + (
@@ -989,7 +992,7 @@
         expand_body(
             inv_ref, stats_ref, zb_ref, params_ref, fast_ref, hidden_ref, low_ref, zc_ref, loads
         )
-        put_forward(out_stats, geo.three(zc_ref[...]), meta_ref[0])
+        put_forward(out_stats, geo.three(zc_ref[...]), meta_ref[0], 0, slow_wide)
 
     hb_two, zc_two, stats, stats_b2 = run(
         expand_two_kernel,
@@ -1026,7 +1029,7 @@
         out_ref.send()
         low_ref[...] = geo.flat(gradient).astype(BF16)
         low_ref.send()
-        put_back(sums_ref, gradient, (zc - mean) * inv)
+        put_back(sums_ref, gradient, (zc - mean) * inv, 0, slow_wide)
 
     outputs, g_two, sums, stats_c2 = run(
         head_kernel,
@@ -1062,8 +1065,8 @@
         edge_ref,
     ):
         limit = meta_ref[0]
-        coeffs = affine(stats_ref, params_ref, inv_ref, slow_wide, 0, wide)
-        both = [back_rows(sums_ref, inv_ref, slow_wide, row, 0, wide) for row in range(2)]
+        coeffs = affine(stats_ref, params_ref, inv_ref, slow_wide, 0, packed)
+        both = [back_rows(sums_ref, inv_ref, slow_wide, row, 0, packed) for row in range(2)]
         gradient = geo.three(g_ref[...].astype(F32))
         gz = norm_back(
             gradient,
@@ -1351,11 +1354,13 @@
         fast_out.send()
         back = geo.three(back)
         masked = jnp.where(mask_groups(back.shape, meta_ref[0]), back, 0.0)
-        mean, inv = moments(stats_c_ref, inv_ref, slow_wide, 0, wide)
-        put_back(sums_out, masked, (geo.three(zc_ref[...].astype(F32)) - mean) * inv)
-        mean, inv = moments(stats_c_ref, inv_ref, slow_wide, wide, wide + slow_wide)
+        mean, inv = moments(stats_c_ref, inv_ref, slow_wide, 0, packed)
+        put_back(
+            sums_out, masked, (geo.three(zc_ref[...].astype(F32)) - mean) * inv, 0, slow_wide
+        )
+        mean, inv = moments(stats_c_ref, inv_ref, slow_wide, packed, packed + slow_wide)
         masked = masked[..., :slow_wide]
-        put_back(sums_out, masked, (geo.three(short_ref[...].astype(F32)) - mean) * inv, wide)
+        put_back(sums_out, masked, (geo.three(short_ref[...].astype(F32)) - mean) * inv, packed)
 
     steps_two, g_one_fast, g_one, sums, sums_a2 = run(
         reduce_back_two_kernel,
@@ -1379,7 +1384,7 @@
         )
         gradient = expand_back_body(*body, loads, gz_ref, g_out, sums_out, message, edge)
         meta_ref, inv_ref, sums_ref, _, stats_ref = body[:5]
-        low, high = wide, wide + slow_wide
+        low, high = packed, packed + slow_wide
         coeffs = affine(stats_ref, short_params_ref, inv_ref, slow_wide, low, high)
         both = [back_rows(sums_ref, inv_ref, slow_wide, row, low, high) for row in range(2)]
         gradient = gradient[..., :slow_wide]
@@ -1602,19 +1607,18 @@
     )
     side_blocks = lax.ppermute(send_blocks, "wa", xor_pairs(2, 1))
 
-    def chip_kernel(own_ref, side_ref, *out_refs):
+    def chip_kernel(side_ref, own_ref, *out_refs):
         for place in range(high):
             total = own_ref[place].astype(F32) + side_ref[place].astype(F32)
             out_refs[place][...] = total.astype(BF16)
             out_refs[place].send()
 
     late_out = ((rows_late, mid), BF16, "hbm")
-    chip_sums = run(chip_kernel, [late_out] * high, saved=(own_blocks, side_blocks))
-    early = jnp.concatenate([sum_space, sum_mid])
-    chip_sums, early = lax.optimization_barrier((chip_sums, early))
+    chip_sums = run(chip_kernel, [late_out] * high, vmem=(side_blocks,), saved=(own_blocks,))
+    chip_sums, early = lax.optimization_barrier((chip_sums, (sum_space, sum_mid)))
     late = [chip_sums[0]] + to_partners(chip_sums[1:], "ha")
     four = lax.axis_size("clips") == 4
-    parts_early = [lax.psum(early, "clips")]
+    early_space, early_mid = lax.psum(early, "clips")
     quarters = clip_parts(meta, [late], 4 if four else 1)
     if four:
         total_late = add_low(quarters[0], *to_partners(quarters[1:], "clips"))
@@ -1693,8 +1697,8 @@
 
     shapes_one = tuple(shard.shape for shard in fast_shards_one)
     shapes_two = tuple(shard.shape for shard in fast_shards_two)
-    groups_early = [
-        (rows_space, [slow_spatial_two.shape, slow_expand_two.shape]),
+    groups_space = [(rows_space, [slow_spatial_two.shape, slow_expand_two.shape])]
+    groups_mid = [
         (
             rows_mid,
             [slow_reduce_two.shape, shapes_two, slow_shortcut_one.shape, slow_expand_one.shape],
@@ -1706,20 +1710,22 @@
             [slow_reduce_one.shape, lateral_weight.shape, slow_spatial_one.shape, shapes_one],
         )
     ]
-    finished = finish((parts_early, groups_early), (parts_late, groups_late))
+    finished = finish(
+        ([early_space], groups_space), ([early_mid], groups_mid), (parts_late, groups_late)
+    )
     grad_slow_spatial_two, grad_slow_expand_two, grad_slow_reduce_two = finished[:3]
     fast_two_grads, (grad_slow_shortcut, grad_slow_expand_one) = finished[3:6], finished[6:8]
     grad_slow_reduce_one, grad_lateral, grad_slow_spatial_one, *fast_one_grads = finished[8:]
 
     def norm_grads(first, second, third):
         slow = [first[:, :mid], second[:, :mid], third[:, :slow_wide]]
-        fast = [first[:, mid:], second[:, mid:], third[:, slow_wide:wide]]
+        fast = [first[:, mid:], second[:, mid:]]
         fast = [jnp.sum(part.reshape(2, PHASES, -1), axis=1) for part in fast]
-        return slow, fast
+        return slow, fast + [third[:, slow_wide:packed]]
 
     slow_one_p, fast_one_p = norm_grads(sums_a1, sums_b1, sums_c1)
     slow_two_p, fast_two_p = norm_grads(sums_a2, sums_b2, sums_c2)
-    grad_slow_norms_one = jnp.concatenate(slow_one_p + [sums_c1[:, wide:]], axis=1)
+    grad_slow_norms_one = jnp.concatenate(slow_one_p + [sums_c1[:, packed:]], axis=1)
     grad_slow_norms_two = jnp.concatenate(slow_two_p, axis=1)
     grad_fast_norms_one = jnp.concatenate(fast_one_p, axis=1)
     grad_fast_norms_two = jnp.concatenate(fast_two_p, axis=1)

time: 394 us -> 388 us (0.985)
  transfers between devices with their start and end apart: 40 -> 40, of which waited for: 22 -> 22; matrix products, arithmetic and copies ran while one was open for 4% -> 3% of each run, Pallas kernels for 15% -> 15%
where the time goes in v1:
time: 388 us; the launch traced here: 386 us
  blocking collectives  120 us (31%)
  waiting for transfers between devices  97 us (25%)
  Pallas kernels  87.7 us (23%)
  starting transfers between devices  45.5 us (12%)
  between operations  16 us (4%)
  local copies, waits for them, and re-layouts  13 us (3%)
  other arithmetic  7.34 us (2%)
    all_to_all x7, blocking collectives, exchange(): return lax.all_to_all(copies, AXES, 0, 0)  90.7 us
    pallas_call x21, Pallas kernels, run(): pl.pallas_call(kernel, out_shape=[jax.ShapeDtypeStruct(shape, dtype) for...  87.7 us
    ppermute x9, waiting for transfers between devices, to_partners(): lax.ppermute(piece, axis, xor_pairs(size, step + 1))  35.9 us
    all_gather x3, waiting for transfers between devices, gather_pack(): return lax.all_gather(jnp.concatenate(parts, axis=0), TILE, axis=0)  19.2 us
    all_to_all x2, blocking collectives, exchange_widest(): lax.all_to_all(jnp.broadcast_to(sums[None], (count,) + sums.shape), TILE,...  16.2 us
    ppermute x9, starting transfers between devices, direct_sum(): lax.ppermute(value, axis, xor_pairs(size, step * times))  14.6 us
    ppermute x9, starting transfers between devices, to_partners(): lax.ppermute(piece, axis, xor_pairs(size, step + 1))  13 us
    all_gather x1, blocking collectives, gather_pack(): return lax.all_gather(jnp.concatenate(parts, axis=0), TILE, axis=0)  12.9 us
  transfers between devices with their start and end apart: 40, of which 22 were waited for; matrix products, arithmetic and copies ran while one was open for 3% of the time, Pallas kernels for 15%

profile of v1, /device:TPU:0, one launch (start us, length us, event | category | flops | bytes accessed | tf_op | source)
XLA Modules:
  0.0 386.4 jit_solution(17823397963400827458)
XLA Ops:
  17.9 12.9 %all-gather = bf16[2688,128]{1,0:T(8,128)(2,1)S(1)} all-gather(bf16[336,128]{1,0:T(8,128)(2,1)S(1)} %fusion.5), channel_id=2, replica_groups=mesh['clips'=4,'ha'=4,'wa'=2] {'ha','wa'}, dimensions={0}, use_global_device_ids=true | all-gather | bytes 774144 | tf_op jit(solution)/shard_map/all_gather | solution.py:526
  37.6 10.2 %all-gather.8.cloned.1.call-done = bf16[6144,256]{1,0:T(8,128)(2,1)} async-done(((bf16[768,256]{1,0:T(8,128)(2,1)}), bf16[6144,256]{1,0:T(8,128)(2,1)}) %all-gather.8.cloned.1.call-update) | async-done | bytes 3145744 | tf_op jit(solution)/shard_map/all_gather | solution.py:526
  59.3 5.6 %collective-permute-done.4.refs_5_ = bf16[128,384]{1,0:T(8,128)(2,1)S(1)} collective-permute-done((bf16[128,384]{1,0:T(8,128)(2,1)S(1)}, bf16[128,384]{1,0:T(8,128)(2,1)S(1)}, u32[]{:S(2)}, u32[]{:S(2)}) %collective-permute-start.4) | collective-permute-done | bytes 98336 | tf_op jit(solution)/shard_map/ppermute | solution.py:454
  68.6 16.8 %all_to_all.60.refs_2_ = f32[32,2,384]{2,1,0:T(2,128)S(1)} all-to-all(f32[32,2,384]{2,1,0:T(2,128)S(1)} %get-tuple-element.151), channel_id=1, replica_groups=mesh['clips'=4,'ha'=4,'wa'=2] {'clips','ha','wa'}, dimensions={0} | all-to-all | bytes 196608 | tf_op jit(solution)/shard_map/all_to_all | solution.py:437
  85.4 9.0 %all-gather.10.cloned.1.call-done = bf16[9216,256]{1,0:T(8,128)(2,1)} async-done(((bf16[1152,256]{1,0:T(8,128)(2,1)}), bf16[9216,256]{1,0:T(8,128)(2,1)}) %all-gather.10.cloned.1.call-update) | async-done | bytes 4718608 | tf_op jit(solution)/shard_map/all_gather | solution.py:526
  109.3 8.2 %all_to_all.61.refs_2_ = f32[8,2,2176]{2,1,0:T(2,128)S(1)} all-to-all(f32[8,2,2176]{2,1,0:T(2,128)S(1)} %broadcast_in_dim.7), channel_id=1, replica_groups=mesh['clips'=4,'ha'=4,'wa'=2] {'ha','wa'}, dimensions={0} | all-to-all | bytes 278528 | tf_op jit(solution)/shard_map/all_to_all | solution.py:444
  135.6 13.7 %all_to_all.62.refs_2_ = f32[32,2,384]{2,1,0:T(2,128)S(1)} all-to-all(f32[32,2,384]{2,1,0:T(2,128)S(1)} %get-tuple-element.169), channel_id=1, replica_groups=mesh['clips'=4,'ha'=4,'wa'=2] {'clips','ha','wa'}, dimensions={0} | all-to-all | bytes 196608 | tf_op jit(solution)/shard_map/all_to_all | solution.py:437
  157.4 10.2 %all-to-all-done.5.refs_2_ = f32[32,2,1152]{2,1,0:T(2,128)S(1)} async-done(((f32[32,2,1152]{2,1,0:T(2,128)}), f32[32,2,1152]{2,1,0:T(2,128)S(1)}, u32[]{:S(2)}, u32[]{:S(2)}) %all-to-all-start.5) | async-done | bytes 294944 | tf_op jit(solution)/shard_map/all_to_all | solution.py:437
  171.3 13.8 %all_to_all.63.refs_2_ = f32[32,2,1152]{2,1,0:T(2,128)} all-to-all(f32[32,2,1152]{2,1,0:T(2,128)S(1)} %get-tuple-element.178), channel_id=1, replica_groups=mesh['clips'=4,'ha'=4,'wa'=2] {'clips','ha','wa'}, dimensions={0} | all-to-all | bytes 589824 | tf_op jit(solution)/shard_map/all_to_all | solution.py:437
  191.4 12.8 %all_to_all.64.refs_2_ = f32[32,2,384]{2,1,0:T(2,128)S(1)} all-to-all(f32[32,2,384]{2,1,0:T(2,128)S(1)} %get-tuple-element.182), channel_id=1, replica_groups=mesh['clips'=4,'ha'=4,'wa'=2] {'clips','ha','wa'}, dimensions={0} | all-to-all | bytes 196608 | tf_op jit(solution)/shard_map/all_to_all | solution.py:437
  204.3 5.6 %shard_map.400 = (bf16[9,192,384]{2,1,0:T(8,128)(2,1)}, f32[192,384]{1,0:T(8,128)}, f32[32,2,384]{2,1,0:T(2,128)S(1)}, f32[2,384]{1,0:T(2,128)S(1)}) custom-call(s32[5]{0:T(128)S(1)} %stack.61.refs_0_, f32[2]{0:T(128)S(1)} %pad_maximum_fusion.20.refs_1_, f32[32,2,384]{2,1,0:T(2,128)S(1)} %all_to_all.64.refs_2_, f32[192,384]{1,0:T(8,128)} %copy-done.14, ...), custom_call_target="tpu_custom_call" | custom-call | flops 2000000000 | bytes 16000000 | tf_op jit(solution)/shard_map/pallas_call | solution.py:202
  213.5 9.6 %all_to_all.65.refs_2_ = f32[32,2,384]{2,1,0:T(2,128)S(1)} all-to-all(f32[32,2,384]{2,1,0:T(2,128)S(1)} %get-tuple-element.187), channel_id=1, replica_groups=mesh['clips'=4,'ha'=4,'wa'=2] {'clips','ha','wa'}, dimensions={0} | all-to-all | bytes 196608 | tf_op jit(solution)/shard_map/all_to_all | solution.py:437
  235.6 8.0 %all_to_all.66.refs_2_ = f32[8,2,2176]{2,1,0:T(2,128)S(1)} all-to-all(f32[8,2,2176]{2,1,0:T(2,128)S(1)} %broadcast_in_dim.8), channel_id=1, replica_groups=mesh['clips'=4,'ha'=4,'wa'=2] {'ha','wa'}, dimensions={0} | all-to-all | bytes 278528 | tf_op jit(solution)/shard_map/all_to_all | solution.py:444
  243.6 5.5 %shard_map.402 = (bf16[192,1536]{1,0:T(8,128)(2,1)}, f32[192,384]{1,0:T(8,128)S(1)}, f32[32,2,384]{2,1,0:T(2,128)S(1)}, bf16[192,768]{1,0:T(8,128)(2,1)}, bf16[6...) custom-call(s32[5]{0:T(128)S(1)} %stack.61.refs_0_, f32[2]{0:T(128)S(1)} %pad_maximum_fusion.20.refs_1_, ...), custom_call_target="tpu_custom_call" | custom-call | flops 2000000000 | bytes 16000000 | tf_op jit(solution)/shard_map/pallas_call | solution.py:202
  249.1 6.4 %shard_map.405 = (bf16[8,1216,256]{2,1,0:T(8,128)(2,1)}, f32[192,1280]{1,0:T(8,128)}) custom-call(bf16[192,1024]{1,0:T(8,128)(2,1)S(1)} %copy-done, bf16[192,256]{1,0:T(8,128)(2,1)S(1)} %get-tuple-element.143.refs_2_.refs_7_.refs_1_.refs_4_, bf16[192,1024]{1,0:T(8,128)(2,1)} %get-tuple-element.201.refs_2_, ...), custom_call_target="tpu_custom_call" | custom-call | flops 2000000000 | bytes 16000000 | tf_op jit(solution)/shard_map/pallas_call | solution.py:202
  258.3 14.3 %all_to_all.67.refs_2_ = f32[32,2,384]{2,1,0:T(2,128)S(1)} all-to-all(f32[32,2,384]{2,1,0:T(2,128)S(1)} %get-tuple-element.193), channel_id=1, replica_groups=mesh['clips'=4,'ha'=4,'wa'=2] {'clips','ha','wa'}, dimensions={0} | all-to-all | bytes 196608 | tf_op jit(solution)/shard_map/all_to_all | solution.py:437
  272.6 5.6 %shard_map.403 = (bf16[9,192,384]{2,1,0:T(8,128)(2,1)}, f32[192,384]{1,0:T(8,128)}, f32[32,2,384]{2,1,0:T(2,128)S(1)}, f32[2,384]{1,0:T(2,128)S(1)}) custom-call(s32[5]{0:T(128)S(1)} %stack.61.refs_0_, f32[2]{0:T(128)S(1)} %pad_maximum_fusion.20.refs_1_, f32[32,2,384]{2,1,0:T(2,128)S(1)} %all_to_all.67.refs_2_, f32[192,384]{1,0:T(8,128)} %copy-done.9, ...), custom_call_target="tpu_custom_call" | custom-call | flops 2000000000 | bytes 16000000 | tf_op jit(solution)/shard_map/pallas_call | solution.py:202
  278.2 9.6 %all_to_all.68.refs_2_ = f32[32,2,384]{2,1,0:T(2,128)S(1)} all-to-all(f32[32,2,384]{2,1,0:T(2,128)S(1)} %get-tuple-element.198), channel_id=1, replica_groups=mesh['clips'=4,'ha'=4,'wa'=2] {'clips','ha','wa'}, dimensions={0} | all-to-all | bytes 196608 | tf_op jit(solution)/shard_map/all_to_all | solution.py:437
  293.8 5.3 %shard_map.407 = (bf16[4,896,256]{2,1,0:T(8,128)(2,1)}, bf16[4,896,256]{2,1,0:T(8,128)(2,1)}) custom-call(s32[5]{0:T(128)S(1)} %stack.61.refs_0_, bf16[3,192,384]{2,1,0:T(8,128)(2,1)} %get-tuple-element.214.refs_1_, bf16[2,192,256]{2,1,0:T(8,128)(2,1)S(1)} %get-tuple-element.215.refs_2_, bf16[192,1024]{1,0:T(8,128)(2,1)} %reshape.174.refs_1_.refs_6_.refs_0_.refs_3_, ...), custom_call_target="tpu_custom_call" | custom-call | flops 2000000000 | bytes 16000000 | tf_op jit(solution)/shard_map/pallas_call | solution.py:202
  317.2 6.6 %collective-permute-done.22.refs_2_ = bf16[896,256]{1,0:T(8,128)(2,1)S(1)} collective-permute-done((bf16[896,256]{1,0:T(8,128)(2,1)S(1)}, bf16[896,256]{1,0:T(8,128)(2,1)S(1)}, u32[]{:S(2)}, u32[]{:S(2)}) %collective-permute-start.22) | collective-permute-done | bytes 458784 | tf_op jit(solution)/shard_map/ppermute | solution.py:611
  323.8 10.1 %collective-permute-done.23.refs_3_ = bf16[896,256]{1,0:T(8,128)(2,1)} collective-permute-done((bf16[896,256]{1,0:T(8,128)(2,1)}, bf16[896,256]{1,0:T(8,128)(2,1)}, u32[]{:S(2)}, u32[]{:S(2)}) %collective-permute-start.23) | collective-permute-done | bytes 458784 | tf_op jit(solution)/shard_map/ppermute | solution.py:611
  342.3 6.1 %collective-permute-done.26 = bf16[224,256]{1,0:T(8,128)(2,1)S(1)} collective-permute-done((bf16[224,256]{1,0:T(8,128)(2,1)S(1)}, bf16[224,256]{1,0:T(8,128)(2,1)S(1)}, u32[]{:S(2)}, u32[]{:S(2)}) %collective-permute-start.26) | collective-permute-done | bytes 114720 | tf_op jit(solution)/shard_map/ppermute | solution.py:611
  360.1 8.5 %collective-permute-done.29.refs_5_ = bf16[224,256]{1,0:T(8,128)(2,1)S(1)} collective-permute-done((bf16[224,256]{1,0:T(8,128)(2,1)S(1)}, bf16[224,256]{1,0:T(8,128)(2,1)S(1)}, u32[]{:S(2)}, u32[]{:S(2)}) %collective-permute-start.29) | collective-permute-done | bytes 114720 | tf_op jit(solution)/shard_map/ppermute | solution.py:611
  368.6 6.0 %all-reduce.5.cloned.1.call-done = (bf16[448,256]{1,0:T(8,128)(2,1)}, bf16[1216,256]{1,0:T(8,128)(2,1)}) async-done(((bf16[448,256]{1,0:T(8,128)(2,1)}, bf16[1216,256]{1,0:T(8,128)(2,1)}), (bf16[448,256]{1,0:T(8,128)(2,1)}, bf16[1216,256]{1,0:T(8,128)(2,1)})) %all-reduce.5.cloned.1.call-update) | async-done | bytes 851984 | tf_op jit(solution)/shard_map/psum | solution.py:1621
  (252 shorter events, 149.9 us)
Async XLA Ops:
  7.2 40.6 %all-gather.8.cloned.1.call-start = ((), (), s32[]{:S(2)}) async-start(), calls=%async_computation.16 | async-start | bytes 3538944 | tf_op jit(solution)/shard_map/all_gather | solution.py:526
  9.1 85.3 %all-gather.10.cloned.1.call-start = ((), (), s32[]{:S(2)}) async-start(), calls=%async_computation.17 | async-start | bytes 5308416 | tf_op jit(solution)/shard_map/all_gather | solution.py:526
  10.5 116.0 %all-gather.12.cloned.1.call-start = ((), (), s32[]{:S(2)}) async-start(), calls=%async_computation.18 | async-start | bytes 1916928 | tf_op jit(solution)/shard_map/all_gather | solution.py:526
  11.2 26.2 %collective-permute-start = (f32[1,128]{1,0:T(1,128)S(1)}, f32[1,128]{1,0:T(1,128)S(1)}, u32[]{:S(2)}, u32[]{:S(2)}) collective-permute-start(f32[1,128]{1,0:T(1,128)S(1)} %broadcast_in_dim.6), channel_id=1, source_target_pairs={{0,16},{8,24},{16,0},{24,8},{1,17},{9,25},{17,1},{25,9},{2,18},{10... | collective-permute-start | bytes 1544 | tf_op jit(solution)/shard_map/ppermute | solution.py:415
  15.3 22.1 %collective-permute-start.1 = (f32[1,128]{1,0:T(1,128)S(1)}, f32[1,128]{1,0:T(1,128)S(1)}, u32[]{:S(2)}, u32[]{:S(2)}) collective-permute-start(f32[1,128]{1,0:T(1,128)S(1)} %broadcast_in_dim.6), channel_id=1, source_target_pairs={{0,8},{8,0},{16,24},{24,16},{1,9},{9,1},{17,25},{25,17},{2,10},{10... | collective-permute-start | bytes 1544 | tf_op jit(solution)/shard_map/ppermute | solution.py:415
  16.9 20.5 %collective-permute-start.2 = (f32[1,128]{1,0:T(1,128)S(1)}, f32[1,128]{1,0:T(1,128)S(1)}, u32[]{:S(2)}, u32[]{:S(2)}) collective-permute-start(f32[1,128]{1,0:T(1,128)S(1)} %broadcast_in_dim.6), channel_id=1, source_target_pairs={{0,24},{8,16},{16,8},{24,0},{1,25},{9,17},{17,9},{25,1},{2,26},{10... | collective-permute-start | bytes 1544 | tf_op jit(solution)/shard_map/ppermute | solution.py:415
  52.0 12.9 %all-to-all-start = ((f32[32,2,384]{2,1,0:T(2,128)}), f32[32,2,384]{2,1,0:T(2,128)S(1)}, u32[]{:S(2)}, u32[]{:S(2)}) async-start(f32[32,2,384]{2,1,0:T(2,128)} %get-tuple-element.145), calls=%async_computation | async-start | bytes 196608 | tf_op jit(solution)/shard_map/all_to_all | solution.py:437
  56.7 8.2 %collective-permute-start.4 = (bf16[128,384]{1,0:T(8,128)(2,1)S(1)}, bf16[128,384]{1,0:T(8,128)(2,1)S(1)}, u32[]{:S(2)}, u32[]{:S(2)}) collective-permute-start(bf16[128,384]{1,0:T(8,128)(2,1)S(1)} %get-tuple-element.269), channel_id=1, source_target_pairs={{0,2},{2,0},{4,6},{6,4},{1,3},{3,1},{5,7},{7,5},{8,10},{10,8},{12,... | collective-permute-start | bytes 294920 | tf_op jit(solution)/shard_map/ppermute | solution.py:454
  121.5 10.4 %all-to-all-start.3 = ((f32[32,2,384]{2,1,0:T(2,128)}), f32[32,2,384]{2,1,0:T(2,128)S(1)}, u32[]{:S(2)}, u32[]{:S(2)}) async-start(f32[32,2,384]{2,1,0:T(2,128)} %get-tuple-element.163), calls=%async_computation.3 | async-start | bytes 196608 | tf_op jit(solution)/shard_map/all_to_all | solution.py:437
  153.5 14.1 %all-to-all-start.5 = ((f32[32,2,1152]{2,1,0:T(2,128)}), f32[32,2,1152]{2,1,0:T(2,128)S(1)}, u32[]{:S(2)}, u32[]{:S(2)}) async-start(f32[32,2,1152]{2,1,0:T(2,128)} %get-tuple-element.173), calls=%async_computation.5 | async-start | bytes 589824 | tf_op jit(solution)/shard_map/all_to_all | solution.py:437
  156.3 153.1 %reduce-scatter.3.cloned.1.call-start = ((), (), s32[]{:S(2)}) async-start(), calls=%async_computation.14 | async-start | bytes 2064384 | tf_op jit(solution)/shard_map/reduce_scatter | solution.py:1297
  190.3 13.9 %collective-permute-start.13 = (bf16[128,768]{1,0:T(8,128)(2,1)S(1)}, bf16[128,768]{1,0:T(8,128)(2,1)S(1)}, u32[]{:S(2)}, u32[]{:S(2)}) collective-permute-start(bf16[128,768]{1,0:T(8,128)(2,1)S(1)} %get-tuple-element.261), channel_id=1, source_target_pairs={{0,2},{2,0},{4,6},{6,4},{1,3},{3,1},{5,7},{7,5},{8,10},{10,8},{12,... | collective-permute-start | bytes 589832 | tf_op jit(solution)/shard_map/ppermute | solution.py:454
  190.8 13.5 %collective-permute-start.14 = (bf16[128,768]{1,0:T(8,128)(2,1)S(1)}, bf16[128,768]{1,0:T(8,128)(2,1)S(1)}, u32[]{:S(2)}, u32[]{:S(2)}) collective-permute-start(bf16[128,768]{1,0:T(8,128)(2,1)S(1)} %get-tuple-element.260), channel_id=1, source_target_pairs={{2,4},{4,2},{3,5},{5,3},{10,12},{12,10},{11,13},{13,11},{18,20},{2... | collective-permute-start | bytes 589832 | tf_op jit(solution)/shard_map/ppermute | solution.py:457
  213.5 96.9 %reduce-scatter.5.cloned.1.call-start = ((), (), s32[]{:S(2)}) async-start(), calls=%async_computation.15 | async-start | bytes 5603328 | tf_op jit(solution)/shard_map/reduce_scatter | solution.py:1455
  255.6 119.0 %all-reduce.5.cloned.1.call-start = ((), (), s32[]{:S(2)}) async-start(), calls=%async_computation.19 | async-start | bytes 1703936 | tf_op jit(solution)/shard_map/psum | solution.py:1621
  257.1 15.6 %collective-permute-start.19 = (bf16[128,768]{1,0:T(8,128)(2,1)S(1)}, bf16[128,768]{1,0:T(8,128)(2,1)S(1)}, u32[]{:S(2)}, u32[]{:S(2)}) collective-permute-start(bf16[128,768]{1,0:T(8,128)(2,1)S(1)} %get-tuple-element.259), channel_id=1, source_target_pairs={{0,2},{2,0},{4,6},{6,4},{1,3},{3,1},{5,7},{7,5},{8,10},{10,8},{12,... | collective-permute-start | bytes 589832 | tf_op jit(solution)/shard_map/ppermute | solution.py:454
  257.7 15.0 %collective-permute-start.20 = (bf16[128,768]{1,0:T(8,128)(2,1)S(1)}, bf16[128,768]{1,0:T(8,128)(2,1)S(1)}, u32[]{:S(2)}, u32[]{:S(2)}) collective-permute-start(bf16[128,768]{1,0:T(8,128)(2,1)S(1)} %get-tuple-element.258), channel_id=1, source_target_pairs={{2,4},{4,2},{3,5},{5,3},{10,12},{12,10},{11,13},{13,11},{18,20},{2... | collective-permute-start | bytes 589832 | tf_op jit(solution)/shard_map/ppermute | solution.py:457
  310.4 13.4 %collective-permute-start.22 = (bf16[896,256]{1,0:T(8,128)(2,1)S(1)}, bf16[896,256]{1,0:T(8,128)(2,1)S(1)}, u32[]{:S(2)}, u32[]{:S(2)}) collective-permute-start(bf16[896,256]{1,0:T(8,128)(2,1)S(1)} %get-tuple-element.229), channel_id=1, source_target_pairs={{0,2},{2,0},{4,6},{6,4},{1,3},{3,1},{5,7},{7,5},{8,10},{10,8},{12,... | collective-permute-start | bytes 1376264 | tf_op jit(solution)/shard_map/ppermute | solution.py:611
  311.8 22.1 %collective-permute-start.23 = (bf16[896,256]{1,0:T(8,128)(2,1)}, bf16[896,256]{1,0:T(8,128)(2,1)}, u32[]{:S(2)}, u32[]{:S(2)}) collective-permute-start(bf16[896,256]{1,0:T(8,128)(2,1)} %get-tuple-element.230), channel_id=1, source_target_pairs={{0,4},{2,6},{4,0},{6,2},{1,5},{3,7},{5,1},{7,3},{8,12},{10,14},{12... | collective-permute-start | bytes 1376264 | tf_op jit(solution)/shard_map/ppermute | solution.py:611
  312.4 21.5 %collective-permute-start.24 = (bf16[896,256]{1,0:T(8,128)(2,1)}, bf16[896,256]{1,0:T(8,128)(2,1)}, u32[]{:S(2)}, u32[]{:S(2)}) collective-permute-start(bf16[896,256]{1,0:T(8,128)(2,1)} %get-tuple-element.231), channel_id=1, source_target_pairs={{0,6},{2,4},{4,2},{6,0},{1,7},{3,5},{5,3},{7,1},{8,14},{10,12},{12... | collective-permute-start | bytes 1376264 | tf_op jit(solution)/shard_map/ppermute | solution.py:611
  337.9 10.5 %collective-permute-start.26 = (bf16[224,256]{1,0:T(8,128)(2,1)S(1)}, bf16[224,256]{1,0:T(8,128)(2,1)S(1)}, u32[]{:S(2)}, u32[]{:S(2)}) collective-permute-start(bf16[224,256]{1,0:T(8,128)(2,1)S(1)} %get-tuple-element.234), channel_id=1, source_target_pairs={{0,16},{8,24},{16,0},{24,8},{1,17},{9,25},{17,1},{25,9},{2,18},{10... | collective-permute-start | bytes 344072 | tf_op jit(solution)/shard_map/ppermute | solution.py:611
  348.5 11.6 %collective-permute-start.28 = (bf16[224,256]{1,0:T(8,128)(2,1)S(1)}, bf16[224,256]{1,0:T(8,128)(2,1)S(1)}, u32[]{:S(2)}, u32[]{:S(2)}) collective-permute-start(bf16[224,256]{1,0:T(8,128)(2,1)S(1)} %add_convert_fusion.refs_3_), channel_id=1, source_target_pairs={{0,8},{8,0},{16,24},{24,16},{1,9},{9,1},{17,25},{25,17},{2,10},{10... | collective-permute-start | bytes 344072 | tf_op jit(solution)/shard_map/ppermute | solution.py:611
  350.3 18.2 %collective-permute-start.29 = (bf16[224,256]{1,0:T(8,128)(2,1)S(1)}, bf16[224,256]{1,0:T(8,128)(2,1)S(1)}, u32[]{:S(2)}, u32[]{:S(2)}) collective-permute-start(bf16[224,256]{1,0:T(8,128)(2,1)S(1)} %add_convert_fusion.refs_3_), channel_id=1, source_target_pairs={{0,16},{8,24},{16,0},{24,8},{1,17},{9,25},{17,1},{25,9},{2,18},{10... | collective-permute-start | bytes 344072 | tf_op jit(solution)/shard_map/ppermute | solution.py:611
  352.1 16.4 %collective-permute-start.30 = (bf16[224,256]{1,0:T(8,128)(2,1)S(1)}, bf16[224,256]{1,0:T(8,128)(2,1)S(1)}, u32[]{:S(2)}, u32[]{:S(2)}) collective-permute-start(bf16[224,256]{1,0:T(8,128)(2,1)S(1)} %add_convert_fusion.refs_3_), channel_id=1, source_target_pairs={{0,24},{8,16},{16,8},{24,0},{1,25},{9,17},{17,9},{25,1},{2,26},{10... | collective-permute-start | bytes 344072 | tf_op jit(solution)/shard_map/ppermute | solution.py:611
  (53 other events, 336.0 us)
Sparse Core Ops, SparseCore 0:
  10.5 37.2 all-gather.7
  50.2 44.1 all-gather.9
  96.9 26.4 all-gather.11
  213.6 36.7 reduce-scatter.2
  255.7 54.6 reduce-scatter.4
  317.3 57.1 all-reduce.4
